TPU v7x, 32 devices: a whole 2x2x4 slice. The times are simulated.
32 devices in a mesh: row: 16 (over z, y, core), col: 2 (over x).
Axes of the slice: x: 2, y: 2, z: 4, core: 2. Of those that a mesh axis runs over, the one named last changes fastest.
Arguments:
- activations: bfloat16 [512, 64, 256], P('row', 'col'), may hold values from -6 to 6
- cotangent: bfloat16 [512, 64, 256], P('row', 'col'), may hold values from -6 to 6
- kernel_wide: float32 [51, 256], replicated, may hold values from -0.875 to 0.875
- kernel_tall: float32 [51, 256], replicated, may hold values from -0.875 to 0.875
- norm_gain: float32 [256], replicated, may hold values from 0.5 to 1.5
- norm_bias: float32 [256], replicated, may hold values from -3 to 3
- weight_in: bfloat16 [256, 1024], replicated, may hold values from -0.375 to 0.375
- bias_in: float32 [1024], replicated, may hold values from -3 to 3
- weight_out: bfloat16 [1024, 256], replicated, may hold values from -0.1875 to 0.1875
- layer_scale: float32 [256], replicated, may hold values from 0.5 to 2
Outputs:
- grad_input: bfloat16 [512, 64, 256], P('row', 'col')
- grad_weight_in: bfloat16 [256, 1024], replicated
- grad_weight_out: bfloat16 [1024, 256], replicated
- grad_kernel_wide: float32 [51, 256], replicated
- grad_kernel_tall: float32 [51, 256], replicated
All inputs are finite; a program needn't handle non-finite values.
Results may differ from a plain program's by a relative error of at most 0.0083.
Values may be sent and summed in bfloat16 or wider, within the bound.
A program may use at most 64 MiB of HBM per device.

v0:
```python
import math

import jax
import jax.numpy as jnp
from jax import lax
from jax.sharding import PartitionSpec as P


def with_halo(block, sides, width):
    for axis, dim in sides:
        count = lax.axis_size(axis)
        forward = [(i, i + 1) for i in range(count - 1)]
        backward = [(target, source) for source, target in forward]
        low = lax.ppermute(
            lax.slice_in_dim(block, block.shape[dim] - width, None, axis=dim), axis, forward
        )
        high = lax.ppermute(lax.slice_in_dim(block, 0, width, axis=dim), axis, backward)
        block = jnp.concatenate([low, block, high], axis=dim)
    return block


def slide_columns(padded, kernel, length):
    total = jnp.zeros((padded.shape[0], length, padded.shape[2]), jnp.float32)
    for offset in range(kernel.shape[0]):
        total = total + kernel[offset] * padded[:, offset : offset + length, :].astype(jnp.float32)
    return total


def slide_rows(padded, kernel, length):
    total = jnp.zeros((length, padded.shape[1], padded.shape[2]), jnp.float32)
    for offset in range(kernel.shape[0]):
        total = total + kernel[offset] * padded[offset : offset + length].astype(jnp.float32)
    return total


def flip_columns(padded, kernel, length):
    last = kernel.shape[0] - 1
    total = jnp.zeros((padded.shape[0], length, padded.shape[2]), jnp.float32)
    for offset in range(kernel.shape[0]):
        total = total + kernel[offset] * padded[
            :, last - offset : last - offset + length, :
        ].astype(jnp.float32)
    return total


def flip_rows(padded, kernel, length):
    last = kernel.shape[0] - 1
    total = jnp.zeros((length, padded.shape[1], padded.shape[2]), jnp.float32)
    for offset in range(kernel.shape[0]):
        total = total + kernel[offset] * padded[last - offset : last - offset + length].astype(
            jnp.float32
        )
    return total


def correlate_columns(grad, padded, taps):
    length = grad.shape[1]
    gradf = grad.astype(jnp.float32)
    return jnp.stack(
        [
            jnp.sum(gradf * padded[:, offset : offset + length, :].astype(jnp.float32), axis=(0, 1))
            for offset in range(taps)
        ]
    )


def correlate_rows(grad, padded, taps):
    length = grad.shape[0]
    gradf = grad.astype(jnp.float32)
    return jnp.stack(
        [
            jnp.sum(gradf * padded[offset : offset + length].astype(jnp.float32), axis=(0, 1))
            for offset in range(taps)
        ]
    )


def gelu_tanh(value):
    return jax.nn.gelu(value, approximate=True)


def mlp_backward(mixed, cot, norm_gain, norm_bias, weight_in, bias_in, weight_out, layer_scale):
    average = jnp.mean(mixed, axis=-1, keepdims=True)
    centred = mixed - average
    spread = jnp.mean(centred * centred, axis=-1, keepdims=True)
    rstd_val = lax.rsqrt(spread + 1e-06)
    unit = centred * rstd_val
    normed = (unit * norm_gain + norm_bias).astype(jnp.bfloat16)
    pre = jnp.dot(normed, weight_in, preferred_element_type=jnp.float32) + bias_in
    lifted_f, pullback = jax.vjp(gelu_tanh, pre)
    lifted = lifted_f.astype(jnp.bfloat16)
    scaled_cot = (layer_scale * cot.astype(jnp.float32)).astype(jnp.bfloat16)
    sum_out = jnp.dot(lifted.T, scaled_cot, preferred_element_type=jnp.float32)
    grad_lift = jnp.dot(scaled_cot, weight_out.T, preferred_element_type=jnp.float32)
    grad_pre = pullback(grad_lift)[0].astype(jnp.bfloat16)
    sum_in = jnp.dot(normed.T, grad_pre, preferred_element_type=jnp.float32)
    grad_unit = jnp.dot(grad_pre, weight_in.T, preferred_element_type=jnp.float32) * norm_gain
    first = jnp.mean(grad_unit, axis=-1, keepdims=True)
    second = jnp.mean(grad_unit * unit, axis=-1, keepdims=True)
    grad_mixed = (rstd_val * (grad_unit - first - unit * second)).astype(jnp.bfloat16)
    return (grad_mixed, sum_in, sum_out)


def local(
    activations,
    cotangent,
    kernel_wide,
    kernel_tall,
    norm_gain,
    norm_bias,
    weight_in,
    bias_in,
    weight_out,
    layer_scale,
):
    tile_rows, tile_cols, chans = activations.shape
    taps = kernel_wide.shape[0]
    reach = taps // 2
    wide_input = with_halo(activations, (("col", 1),), reach)
    hidden = slide_columns(wide_input, kernel_wide, tile_cols).astype(jnp.bfloat16)
    tall_hidden = with_halo(hidden, (("row", 0),), reach)
    mixed = slide_rows(tall_hidden, kernel_tall, tile_rows)
    grad_flat, sum_in, sum_out = mlp_backward(
        mixed.reshape(-1, chans),
        cotangent.reshape(-1, chans),
        norm_gain,
        norm_bias,
        weight_in,
        bias_in,
        weight_out,
        layer_scale,
    )
    grad_mixed = grad_flat.reshape(tile_rows, tile_cols, chans)
    tall_grad = with_halo(grad_mixed, (("row", 0),), reach)
    grad_hidden = flip_rows(tall_grad, kernel_tall, tile_rows).astype(jnp.bfloat16)
    wide_grad = with_halo(grad_hidden, (("col", 1),), reach)
    grad_input = (
        cotangent.astype(jnp.float32) + flip_columns(wide_grad, kernel_wide, tile_cols)
    ).astype(jnp.bfloat16)
    part_tall = correlate_rows(grad_mixed, tall_hidden, taps)
    part_wide = correlate_columns(grad_hidden, wide_input, taps)
    pixels = tile_rows * lax.axis_size("row") * tile_cols * lax.axis_size("col")
    factor = 1.0 / math.sqrt(pixels)
    total_in, total_out, total_wide, total_tall = lax.psum(
        (sum_in, sum_out, part_wide, part_tall), ("row", "col")
    )
    grad_in = (total_in * factor).astype(jnp.bfloat16)
    grad_out = (total_out * factor).astype(jnp.bfloat16)
    return (grad_input, grad_in, grad_out, total_wide * factor, total_tall * factor)


def solution(mesh):
    in_specs = (
        P("row", "col", None),
        P("row", "col", None),
        P(),
        P(),
        P(),
        P(),
        P(),
        P(),
        P(),
        P(),
    )
    out_specs = (P("row", "col", None), P(), P(), P(), P())
    return jax.shard_map(local, mesh=mesh, in_specs=in_specs, out_specs=out_specs, check_vma=False)
```

profile of v0, /device:TPU:0, one launch (start us, length us, event | category | flops | bytes accessed | tf_op | source)
XLA Modules:
  0.0 421.1 jit_solution(11148134464705375283)
XLA Ops:
  7.2 0.0 copy-start
  7.2 0.0 all-reduce.5.cloned.1.call-start
  7.2 1.5 fusion.441
  8.8 4.9 %collective-permute-start = (bf16[32,25,256]{2,1,0:T(8,128)(2,1)S(1)}, bf16[32,25,256]{2,1,0:T(8,128)(2,1)S(1)}, u32[]{:S(2)}, u32[]{:S(2)}) collective-permute-start(bf16[32,25,256]{2,1,0:T(8,128)(2,1)S(1)} %get-tuple-element.123), channel_id=1, source_target_pairs={{0,1},{2,3},{4,5},{6,7},{8,9},{10,11},{12,13},{14,15},{16,17},{18,... | collective-permute-start | bytes 1228808 | tf_op jit(solution)/shard_map/ppermute | solution.py:14
  13.7 1.3 collective-permute-start.1
  15.0 1.0 fusion.445
  16.2 1.0 fusion.446
  17.4 1.7 fusion.442
  19.1 1.6 fusion.447
  20.6 1.1 constant_dynamic-update-slice_fusion.1
  21.7 1.7 fusion.443
  23.4 5.5 %collective-permute-done.1 = bf16[32,25,256]{2,1,0:T(8,128)(2,1)S(1)} collective-permute-done((bf16[32,25,256]{2,1,0:T(8,128)(2,1)S(1)}, bf16[32,25,256]{2,1,0:T(8,128)(2,1)S(1)}, u32[]{:S(2)}, u32[]{:S(2)}) %collective-permute-start.1) | collective-permute-done | bytes 409632 | tf_op jit(solution)/shard_map/ppermute | solution.py:17
  29.0 0.0 copy-start.118
  29.0 11.3 %fusion.262 = bf16[32,32,256]{2,1,0:T(8,128)(2,1)S(1)} fusion(bf16[32,32,256]{2,1,0:T(8,128)(2,1)S(1)} %copy-done.1, f32[256]{0:T(256)} %bitcast.51, f32[256]{0:T(256)} %bitcast.50, f32[256]{0:T(256)S(1)} %bitcast.285, f32[256]{0:T(256)S(1)} %bitcast.287, f32[256]{0:T(256)S(1)} %bitcast.289, f32[256]{0:T(256)S(1)} %bitcast.291, f32[256]{0:T(256)S(1)} %bitcast.293, ...), kind=kLoop, calls=%fused_computation.818 | loop fusion | flops 59768832 | bytes 14617600 | tf_op jit(solution)/shard_map/convert_element_type | solution.py:120
  40.7 0.1 fusion.440
  40.8 1.3 collective-permute-start.2
  42.2 1.5 collective-permute-start.3
  43.6 0.9 fusion.444
  44.7 0.9 fusion.261
  45.6 1.9 collective-permute-done.3
  47.5 13.4 %fusion.436 = (f32[32,32]{1,0:T(8,128)S(1)}, f32[32,32,256]{2,1,0:T(8,128)}) fusion(bf16[25,32,256]{2,1,0:T(8,128)(2,1)S(1)} %collective-permute-done.3, bf16[32,32,256]{2,1,0:T(8,128)(2,1)S(1)} %fusion.262, f32[256]{0:T(256)S(1)} %bitcast.381, f32[256]{0:T(256)S(1)} %bitcast.383, f32[256]{0:T(256)} %bitcast.99, f32[256]{0:T(256)} %bitcast.98, ...), kind=kLoop, calls=%fused_computation.1007 | loop fusion | flops 53214208 | bytes 2448384 | tf_op jit(solution)/shard_map/reduce_sum | solution.py:83
  61.0 0.1 div.16
  61.1 1.6 multiply_reduce_fusion.1
  62.7 0.1 rsqrt.12
  62.8 1.6 add_convert_fusion.2
  64.4 0.0 copy-start.6
  64.4 0.8 copy-done.6
  65.2 0.7 fusion.448
  65.9 0.3 copy-done.13
  66.2 0.2 copy-done.121
  66.4 3.3 fusion.6
  69.7 0.9 fusion.435
  70.6 0.4 copy-done.9
  71.0 8.1 %fusion.182 = (f32[256]{0:T(256)}, f32[256]{0:T(256)}, f32[256]{0:T(256)}, f32[256]{0:T(256)}, f32[256]{0:T(256)}, /*index=5*/f32[256]{0:T(256)}, f32[256]{0:T(2...) fusion(bf16[25,32,256]{2,1,0:T(8,128)(2,1)S(1)} %copy-done.9, bf16[32,32,256]{2,1,0:T(8,128)(2,1)S(1)} %fusion.262, ...), kind=kLoop, calls=%fused_computation.728 | loop fusion | flops 11532032 | bytes 3580928 | tf_op jit(solution)/shard_map/reduce_sum | solution.py:72
  79.1 1.0 fusion.439
  80.1 8.8 %collective-permute-start.5 = (bf16[25,32,256]{2,1,0:T(8,128)(2,1)}, bf16[25,32,256]{2,1,0:T(8,128)(2,1)}, u32[]{:S(2)}, u32[]{:S(2)}) collective-permute-start(bf16[25,32,256]{2,1,0:T(8,128)(2,1)} %bitcast.106), channel_id=1, source_target_pairs={{0,2},{2,4},{4,6},{6,8},{8,10},{10,12},{12,14},{14,16},{16,18},{18... | collective-permute-start | bytes 1228808 | tf_op jit(solution)/shard_map/ppermute | solution.py:14
  88.8 1.3 collective-permute-start.4
  90.1 1.7 fusion.147
  91.8 1.8 fusion.173
  93.6 1.9 fusion.183
  95.5 1.9 fusion.157
  97.5 1.9 fusion.156
  99.4 9.2 %stack.415 = f32[51,256]{1,0:T(8,128)} concatenate(f32[1,256]{1,0:T(1,128)} %bitcast.409, f32[1,256]{1,0:T(1,128)} %bitcast.410, f32[1,256]{1,0:T(1,128)} %bitcast.411, f32[1,256]{1,0:T(1,128)} %bitcast.412, f32[1,256]{1,0:T(1,128)} %bitcast.413, f32[1,256]{1,0:T(1,128)} %bitcast.414, f32[1,256]{1,0:T(1,128)} %bitcast.415, f32[1,256]{1,0:T(1,128)} %bitcast.416, ...), dimensions={0} | concatenate | bytes 104448 | tf_op jit(solution)/shard_map/stack | solution.py:70
  108.7 5.0 %fusion.7 = f32[1024,256]{1,0:T(8,128)} fusion(bf16[1024,256]{1,0:T(8,128)(2,1)} %fusion.261, f32[1024,1024]{1,0:T(8,128)} %copy-done.3, f32[1024]{0:T(1024)} %param.17), kind=kOutput, calls=%fused_computation.450 | convolution fusion | flops 547356672 | bytes 5771264 | tf_op jit(solution)/shard_map/dot_general | solution.py:93
  113.8 19.6 %fusion.258 = (f32[256]{0:T(256)S(1)}, f32[256]{0:T(256)S(1)}, f32[256]{0:T(256)S(1)}, f32[256]{0:T(256)S(1)}, f32[256]{0:T(256)S(1)}, /*index=5*/f32[256]{0:T(2...) fusion(bf16[32,57,256]{2,1,0:T(8,128)(2,1)S(1)} %constant_dynamic-update-slice_fusion, ...), kind=kLoop, calls=%fused_computation.804 | loop fusion | flops 58980608 | bytes 5597184 | tf_op jit(solution)/shard_map/reduce_sum | solution.py:61
  133.4 2.7 fusion.259
  136.2 1.7 fusion.231
  137.8 2.0 fusion.233
  139.8 1.9 fusion.232
  142.1 4.3 %stack.363 = f32[51,256]{1,0:T(8,128)} concatenate(f32[1,256]{1,0:T(1,128)S(1)} %bitcast.432, f32[1,256]{1,0:T(1,128)S(1)} %bitcast.431, f32[1,256]{1,0:T(1,128)S(1)} %bitcast.429, f32[1,256]{1,0:T(1,128)S(1)} %bitcast.430, f32[1,256]{1,0:T(1,128)S(1)} %bitcast.443, f32[1,256]{1,0:T(1,128)S(1)} %bitcast.444, f32[1,256]{1,0:T(1,128)S(1)} %bitcast.445, f32[1,256]{1,0:T(1,128)S(1)} %bitcast.446, ...), dimensions={0} | concatenate | bytes 104448 | tf_op jit(solution)/shard_map/stack | solution.py:59
  146.4 0.0 all-reduce.5.cloned.1.call-update
  146.5 0.3 all-reduce.7.cloned.1.call-start
  146.8 3.3 fusion.449
  150.1 0.0 all-reduce.7.cloned.1.call-update
  150.1 1.1 fusion.438
  151.2 1.3 collective-permute-start.6
  152.5 4.6 %collective-permute-start.7 = (bf16[32,25,256]{2,1,0:T(8,128)(2,1)S(1)}, bf16[32,25,256]{2,1,0:T(8,128)(2,1)S(1)}, u32[]{:S(2)}, u32[]{:S(2)}) collective-permute-start(bf16[32,25,256]{2,1,0:T(8,128)(2,1)S(1)} %get-tuple-element.118), channel_id=1, source_target_pairs={{0,1},{2,3},{4,5},{6,7},{8,9},{10,11},{12,13},{14,15},{16,17},{18,... | collective-permute-start | bytes 1228808 | tf_op jit(solution)/shard_map/ppermute | solution.py:14
  157.1 112.5 %all-reduce.5.cloned.1.call-done = (f32[51,256]{1,0:T(8,128)}, f32[51,256]{1,0:T(8,128)}) async-done(((f32[51,256]{1,0:T(8,128)}, f32[51,256]{1,0:T(8,128)}), (f32[51,256]{1,0:T(8,128)}, f32[51,256]{1,0:T(8,128)})) %all-reduce.5.cloned.1.call-update) | async-done | bytes 104464 | tf_op jit(solution)/shard_map/psum | solution.py:144
  269.7 1.4 broadcast_multiply_fusion.1
  271.1 1.4 broadcast_multiply_fusion
  272.9 12.9 %add_convert_fusion = bf16[32,32,256]{2,1,0:T(8,128)(2,1)} fusion(bf16[32,32,256]{2,1,0:T(8,128)(2,1)S(1)} %get-tuple-element.114, bf16[32,25,256]{2,1,0:T(8,128)(2,1)S(1)} %collective-permute-done.7, bf16[32,25,256]{2,1,0:T(8,128)(2,1)S(1)} %collective-permute-done.6, f32[256]{0:T(256)} %bitcast.51, f32[256]{0:T(256)} %bitcast.50, f32[256]{0:T(256)S(1)} %bitcast.286, ...), kind=kLoop, calls=%fused_computation.812 | loop fusion | flops 79953920 | bytes 2444288 | tf_op jit(solution)/shard_map/convert_element_type | solution.py:139
  285.9 124.1 %all-reduce.7.cloned.1.call-done = (f32[256,1024]{1,0:T(8,128)}, f32[1024,256]{1,0:T(8,128)}) async-done(((f32[256,1024]{1,0:T(8,128)}, f32[1024,256]{1,0:T(8,128)}), (f32[256,1024]{1,0:T(8,128)}, f32[1024,256]{1,0:T(8,128)})) %all-reduce.7.cloned.1.call-update) | async-done | bytes 2097168 | tf_op jit(solution)/shard_map/psum | solution.py:144
  410.0 2.1 multiply_convert_fusion.3
  412.1 2.1 multiply_convert_fusion.2
  (249 shorter events, 0.6 us)
Async XLA Ops:
  7.2 58.0 %copy-start = (bf16[256,1024]{1,0:T(8,128)(2,1)S(1)}, bf16[256,1024]{1,0:T(8,128)(2,1)}, u32[]{:S(2)}) copy-start(bf16[256,1024]{1,0:T(8,128)(2,1)} %param.16) | copy-start | bytes 1572868
  7.2 262.5 %all-reduce.5.cloned.1.call-start = ((), (), s32[]{:S(2)}) async-start(), calls=%async_computation | async-start | bytes 229376 | tf_op jit(solution)/shard_map/psum | solution.py:144
  8.8 20.2 %collective-permute-start = (bf16[32,25,256]{2,1,0:T(8,128)(2,1)S(1)}, bf16[32,25,256]{2,1,0:T(8,128)(2,1)S(1)}, u32[]{:S(2)}, u32[]{:S(2)}) collective-permute-start(bf16[32,25,256]{2,1,0:T(8,128)(2,1)S(1)} %get-tuple-element.123), channel_id=1, source_target_pairs={{0,1},{2,3},{4,5},{6,7},{8,9},{10,11},{12,13},{14,15},{16,17},{18,... | collective-permute-start | bytes 1228808 | tf_op jit(solution)/shard_map/ppermute | solution.py:14
  13.7 15.3 %collective-permute-start.1 = (bf16[32,25,256]{2,1,0:T(8,128)(2,1)S(1)}, bf16[32,25,256]{2,1,0:T(8,128)(2,1)S(1)}, u32[]{:S(2)}, u32[]{:S(2)}) collective-permute-start(bf16[32,25,256]{2,1,0:T(8,128)(2,1)S(1)} %get-tuple-element.124), channel_id=1, source_target_pairs={{1,0},{3,2},{5,4},{7,6},{9,8},{11,10},{13,12},{15,14},{17,16},{19,... | collective-permute-start | bytes 1228808 | tf_op jit(solution)/shard_map/ppermute | solution.py:17
  16.0 24.3 %copy-start.16 = (f32[1,256]{1,0:T(1,128)}, f32[1,256]{1,0:T(1,128)S(1)}, u32[]{:S(2)}) copy-start(f32[1,256]{1,0:T(1,128)S(1)} %get-tuple-element.176) | copy-start | bytes 3076
  16.0 24.3 %copy-start.18 = (f32[1,256]{1,0:T(1,128)}, f32[1,256]{1,0:T(1,128)S(1)}, u32[]{:S(2)}) copy-start(f32[1,256]{1,0:T(1,128)S(1)} %get-tuple-element.177) | copy-start | bytes 3076
  16.0 24.3 %copy-start.20 = (f32[1,256]{1,0:T(1,128)}, f32[1,256]{1,0:T(1,128)S(1)}, u32[]{:S(2)}) copy-start(f32[1,256]{1,0:T(1,128)S(1)} %get-tuple-element.178) | copy-start | bytes 3076
  16.0 24.3 %copy-start.22 = (f32[1,256]{1,0:T(1,128)}, f32[1,256]{1,0:T(1,128)S(1)}, u32[]{:S(2)}) copy-start(f32[1,256]{1,0:T(1,128)S(1)} %get-tuple-element.179) | copy-start | bytes 3076
  16.0 24.3 %copy-start.24 = (f32[1,256]{1,0:T(1,128)}, f32[1,256]{1,0:T(1,128)S(1)}, u32[]{:S(2)}) copy-start(f32[1,256]{1,0:T(1,128)S(1)} %get-tuple-element.180) | copy-start | bytes 3076
  16.0 24.3 %copy-start.26 = (f32[1,256]{1,0:T(1,128)}, f32[1,256]{1,0:T(1,128)S(1)}, u32[]{:S(2)}) copy-start(f32[1,256]{1,0:T(1,128)S(1)} %get-tuple-element.181) | copy-start | bytes 3076
  16.0 24.3 %copy-start.28 = (f32[1,256]{1,0:T(1,128)}, f32[1,256]{1,0:T(1,128)S(1)}, u32[]{:S(2)}) copy-start(f32[1,256]{1,0:T(1,128)S(1)} %get-tuple-element.182) | copy-start | bytes 3076
  16.0 24.3 %copy-start.30 = (f32[1,256]{1,0:T(1,128)}, f32[1,256]{1,0:T(1,128)S(1)}, u32[]{:S(2)}) copy-start(f32[1,256]{1,0:T(1,128)S(1)} %get-tuple-element.183) | copy-start | bytes 3076
  16.1 24.3 %copy-start.32 = (f32[1,256]{1,0:T(1,128)}, f32[1,256]{1,0:T(1,128)S(1)}, u32[]{:S(2)}) copy-start(f32[1,256]{1,0:T(1,128)S(1)} %get-tuple-element.184) | copy-start | bytes 3076
  16.1 24.3 %copy-start.34 = (f32[1,256]{1,0:T(1,128)}, f32[1,256]{1,0:T(1,128)S(1)}, u32[]{:S(2)}) copy-start(f32[1,256]{1,0:T(1,128)S(1)} %get-tuple-element.185) | copy-start | bytes 3076
  16.1 24.3 %copy-start.36 = (f32[1,256]{1,0:T(1,128)}, f32[1,256]{1,0:T(1,128)S(1)}, u32[]{:S(2)}) copy-start(f32[1,256]{1,0:T(1,128)S(1)} %get-tuple-element.186) | copy-start | bytes 3076
  16.1 24.3 %copy-start.38 = (f32[1,256]{1,0:T(1,128)}, f32[1,256]{1,0:T(1,128)S(1)}, u32[]{:S(2)}) copy-start(f32[1,256]{1,0:T(1,128)S(1)} %get-tuple-element.187) | copy-start | bytes 3076
  16.1 24.3 %copy-start.40 = (f32[1,256]{1,0:T(1,128)}, f32[1,256]{1,0:T(1,128)S(1)}, u32[]{:S(2)}) copy-start(f32[1,256]{1,0:T(1,128)S(1)} %get-tuple-element.188) | copy-start | bytes 3076
  16.1 24.3 %copy-start.42 = (f32[1,256]{1,0:T(1,128)}, f32[1,256]{1,0:T(1,128)S(1)}, u32[]{:S(2)}) copy-start(f32[1,256]{1,0:T(1,128)S(1)} %get-tuple-element.189) | copy-start | bytes 3076
  40.8 4.8 %collective-permute-start.2 = (bf16[25,32,256]{2,1,0:T(8,128)(2,1)S(1)}, bf16[25,32,256]{2,1,0:T(8,128)(2,1)S(1)}, u32[]{:S(2)}, u32[]{:S(2)}) collective-permute-start(bf16[25,32,256]{2,1,0:T(8,128)(2,1)S(1)} %get-tuple-element.121), channel_id=1, source_target_pairs={{0,2},{2,4},{4,6},{6,8},{8,10},{10,12},{12,14},{14,16},{16,18},{18... | collective-permute-start | bytes 1228808 | tf_op jit(solution)/shard_map/ppermute | solution.py:14
  42.2 5.4 %collective-permute-start.3 = (bf16[25,32,256]{2,1,0:T(8,128)(2,1)S(1)}, bf16[25,32,256]{2,1,0:T(8,128)(2,1)S(1)}, u32[]{:S(2)}, u32[]{:S(2)}) collective-permute-start(bf16[25,32,256]{2,1,0:T(8,128)(2,1)S(1)} %get-tuple-element.122), channel_id=1, source_target_pairs={{2,0},{4,2},{6,4},{8,6},{10,8},{12,10},{14,12},{16,14},{18,16},{20... | collective-permute-start | bytes 1228808 | tf_op jit(solution)/shard_map/ppermute | solution.py:17
  80.1 33.6 %collective-permute-start.5 = (bf16[25,32,256]{2,1,0:T(8,128)(2,1)}, bf16[25,32,256]{2,1,0:T(8,128)(2,1)}, u32[]{:S(2)}, u32[]{:S(2)}) collective-permute-start(bf16[25,32,256]{2,1,0:T(8,128)(2,1)} %bitcast.106), channel_id=1, source_target_pairs={{0,2},{2,4},{4,6},{6,8},{8,10},{10,12},{12,14},{14,16},{16,18},{18... | collective-permute-start | bytes 1228808 | tf_op jit(solution)/shard_map/ppermute | solution.py:14
  88.8 24.8 %collective-permute-start.4 = (bf16[25,32,256]{2,1,0:T(8,128)(2,1)}, bf16[25,32,256]{2,1,0:T(8,128)(2,1)}, u32[]{:S(2)}, u32[]{:S(2)}) collective-permute-start(bf16[25,32,256]{2,1,0:T(8,128)(2,1)} %bitcast.105), channel_id=1, source_target_pairs={{2,0},{4,2},{6,4},{8,6},{10,8},{12,10},{14,12},{16,14},{18,16},{20... | collective-permute-start | bytes 1228808 | tf_op jit(solution)/shard_map/ppermute | solution.py:17
  141.7 130.8 %copy-start.12 = (bf16[32,32,256]{2,1,0:T(8,128)(2,1)S(1)}, bf16[32,32,256]{2,1,0:T(8,128)(2,1)}, u32[]{:S(2)}) copy-start(bf16[32,32,256]{2,1,0:T(8,128)(2,1)} %param.11) | copy-start | bytes 1572868
  141.7 130.8 %copy-start.17 = (f32[1,256]{1,0:T(1,128)S(1)}, f32[1,256]{1,0:T(1,128)}, u32[]{:S(2)}) copy-start(f32[1,256]{1,0:T(1,128)} %copy-done.16) | copy-start | bytes 3076
  141.8 130.8 %copy-start.19 = (f32[1,256]{1,0:T(1,128)S(1)}, f32[1,256]{1,0:T(1,128)}, u32[]{:S(2)}) copy-start(f32[1,256]{1,0:T(1,128)} %copy-done.18) | copy-start | bytes 3076
  141.8 130.8 %copy-start.21 = (f32[1,256]{1,0:T(1,128)S(1)}, f32[1,256]{1,0:T(1,128)}, u32[]{:S(2)}) copy-start(f32[1,256]{1,0:T(1,128)} %copy-done.20) | copy-start | bytes 3076
  141.8 130.8 %copy-start.23 = (f32[1,256]{1,0:T(1,128)S(1)}, f32[1,256]{1,0:T(1,128)}, u32[]{:S(2)}) copy-start(f32[1,256]{1,0:T(1,128)} %copy-done.22) | copy-start | bytes 3076
  141.8 130.8 %copy-start.25 = (f32[1,256]{1,0:T(1,128)S(1)}, f32[1,256]{1,0:T(1,128)}, u32[]{:S(2)}) copy-start(f32[1,256]{1,0:T(1,128)} %copy-done.24) | copy-start | bytes 3076
  141.8 130.8 %copy-start.27 = (f32[1,256]{1,0:T(1,128)S(1)}, f32[1,256]{1,0:T(1,128)}, u32[]{:S(2)}) copy-start(f32[1,256]{1,0:T(1,128)} %copy-done.26) | copy-start | bytes 3076
  141.8 130.8 %copy-start.29 = (f32[1,256]{1,0:T(1,128)S(1)}, f32[1,256]{1,0:T(1,128)}, u32[]{:S(2)}) copy-start(f32[1,256]{1,0:T(1,128)} %copy-done.28) | copy-start | bytes 3076
  141.8 130.8 %copy-start.31 = (f32[1,256]{1,0:T(1,128)S(1)}, f32[1,256]{1,0:T(1,128)}, u32[]{:S(2)}) copy-start(f32[1,256]{1,0:T(1,128)} %copy-done.30) | copy-start | bytes 3076
  141.8 130.8 %copy-start.33 = (f32[1,256]{1,0:T(1,128)S(1)}, f32[1,256]{1,0:T(1,128)}, u32[]{:S(2)}) copy-start(f32[1,256]{1,0:T(1,128)} %copy-done.32) | copy-start | bytes 3076
  141.8 130.8 %copy-start.35 = (f32[1,256]{1,0:T(1,128)S(1)}, f32[1,256]{1,0:T(1,128)}, u32[]{:S(2)}) copy-start(f32[1,256]{1,0:T(1,128)} %copy-done.34) | copy-start | bytes 3076
  141.8 130.8 %copy-start.37 = (f32[1,256]{1,0:T(1,128)S(1)}, f32[1,256]{1,0:T(1,128)}, u32[]{:S(2)}) copy-start(f32[1,256]{1,0:T(1,128)} %copy-done.36) | copy-start | bytes 3076
  141.9 130.8 %copy-start.39 = (f32[1,256]{1,0:T(1,128)S(1)}, f32[1,256]{1,0:T(1,128)}, u32[]{:S(2)}) copy-start(f32[1,256]{1,0:T(1,128)} %copy-done.38) | copy-start | bytes 3076
  141.9 130.8 %copy-start.41 = (f32[1,256]{1,0:T(1,128)S(1)}, f32[1,256]{1,0:T(1,128)}, u32[]{:S(2)}) copy-start(f32[1,256]{1,0:T(1,128)} %copy-done.40) | copy-start | bytes 3076
  141.9 130.8 %copy-start.43 = (f32[1,256]{1,0:T(1,128)S(1)}, f32[1,256]{1,0:T(1,128)}, u32[]{:S(2)}) copy-start(f32[1,256]{1,0:T(1,128)} %copy-done.42) | copy-start | bytes 3076
  141.9 130.8 %copy-start.45 = (f32[1,256]{1,0:T(1,128)S(1)}, f32[1,256]{1,0:T(1,128)}, u32[]{:S(2)}) copy-start(f32[1,256]{1,0:T(1,128)} %copy-done.44) | copy-start | bytes 3076
  141.9 130.8 %copy-start.47 = (f32[1,256]{1,0:T(1,128)S(1)}, f32[1,256]{1,0:T(1,128)}, u32[]{:S(2)}) copy-start(f32[1,256]{1,0:T(1,128)} %copy-done.46) | copy-start | bytes 3076
  141.9 130.8 %copy-start.49 = (f32[1,256]{1,0:T(1,128)S(1)}, f32[1,256]{1,0:T(1,128)}, u32[]{:S(2)}) copy-start(f32[1,256]{1,0:T(1,128)} %copy-done.48) | copy-start | bytes 3076
  141.9 130.8 %copy-start.51 = (f32[1,256]{1,0:T(1,128)S(1)}, f32[1,256]{1,0:T(1,128)}, u32[]{:S(2)}) copy-start(f32[1,256]{1,0:T(1,128)} %copy-done.50) | copy-start | bytes 3076
  141.9 130.8 %copy-start.53 = (f32[1,256]{1,0:T(1,128)S(1)}, f32[1,256]{1,0:T(1,128)}, u32[]{:S(2)}) copy-start(f32[1,256]{1,0:T(1,128)} %copy-done.52) | copy-start | bytes 3076
  141.9 130.8 %copy-start.55 = (f32[1,256]{1,0:T(1,128)S(1)}, f32[1,256]{1,0:T(1,128)}, u32[]{:S(2)}) copy-start(f32[1,256]{1,0:T(1,128)} %copy-done.54) | copy-start | bytes 3076
  141.9 130.8 %copy-start.57 = (f32[1,256]{1,0:T(1,128)S(1)}, f32[1,256]{1,0:T(1,128)}, u32[]{:S(2)}) copy-start(f32[1,256]{1,0:T(1,128)} %copy-done.56) | copy-start | bytes 3076
  142.0 130.8 %copy-start.59 = (f32[1,256]{1,0:T(1,128)S(1)}, f32[1,256]{1,0:T(1,128)}, u32[]{:S(2)}) copy-start(f32[1,256]{1,0:T(1,128)} %copy-done.58) | copy-start | bytes 3076
  142.0 130.8 %copy-start.61 = (f32[1,256]{1,0:T(1,128)S(1)}, f32[1,256]{1,0:T(1,128)}, u32[]{:S(2)}) copy-start(f32[1,256]{1,0:T(1,128)} %copy-done.60) | copy-start | bytes 3076
  142.0 130.8 %copy-start.63 = (f32[1,256]{1,0:T(1,128)S(1)}, f32[1,256]{1,0:T(1,128)}, u32[]{:S(2)}) copy-start(f32[1,256]{1,0:T(1,128)} %copy-done.62) | copy-start | bytes 3076
  142.0 130.8 %copy-start.65 = (f32[1,256]{1,0:T(1,128)S(1)}, f32[1,256]{1,0:T(1,128)}, u32[]{:S(2)}) copy-start(f32[1,256]{1,0:T(1,128)} %copy-done.64) | copy-start | bytes 3076
  142.0 130.8 %copy-start.67 = (f32[1,256]{1,0:T(1,128)S(1)}, f32[1,256]{1,0:T(1,128)}, u32[]{:S(2)}) copy-start(f32[1,256]{1,0:T(1,128)} %copy-done.66) | copy-start | bytes 3076
  142.0 130.8 %copy-start.69 = (f32[1,256]{1,0:T(1,128)S(1)}, f32[1,256]{1,0:T(1,128)}, u32[]{:S(2)}) copy-start(f32[1,256]{1,0:T(1,128)} %copy-done.68) | copy-start | bytes 3076
  142.0 130.8 %copy-start.71 = (f32[1,256]{1,0:T(1,128)S(1)}, f32[1,256]{1,0:T(1,128)}, u32[]{:S(2)}) copy-start(f32[1,256]{1,0:T(1,128)} %copy-done.70) | copy-start | bytes 3076
  142.0 130.8 %copy-start.73 = (f32[1,256]{1,0:T(1,128)S(1)}, f32[1,256]{1,0:T(1,128)}, u32[]{:S(2)}) copy-start(f32[1,256]{1,0:T(1,128)} %copy-done.72) | copy-start | bytes 3076
  142.0 130.8 %copy-start.75 = (f32[1,256]{1,0:T(1,128)S(1)}, f32[1,256]{1,0:T(1,128)}, u32[]{:S(2)}) copy-start(f32[1,256]{1,0:T(1,128)} %copy-done.74) | copy-start | bytes 3076
  142.0 130.8 %copy-start.77 = (f32[1,256]{1,0:T(1,128)S(1)}, f32[1,256]{1,0:T(1,128)}, u32[]{:S(2)}) copy-start(f32[1,256]{1,0:T(1,128)} %copy-done.76) | copy-start | bytes 3076
  142.1 130.8 %copy-start.79 = (f32[1,256]{1,0:T(1,128)S(1)}, f32[1,256]{1,0:T(1,128)}, u32[]{:S(2)}) copy-start(f32[1,256]{1,0:T(1,128)} %copy-done.78) | copy-start | bytes 3076
  142.1 130.8 %copy-start.81 = (f32[1,256]{1,0:T(1,128)S(1)}, f32[1,256]{1,0:T(1,128)}, u32[]{:S(2)}) copy-start(f32[1,256]{1,0:T(1,128)} %copy-done.80) | copy-start | bytes 3076
  142.1 130.8 %copy-start.83 = (f32[1,256]{1,0:T(1,128)S(1)}, f32[1,256]{1,0:T(1,128)}, u32[]{:S(2)}) copy-start(f32[1,256]{1,0:T(1,128)} %copy-done.82) | copy-start | bytes 3076
  142.1 130.8 %copy-start.85 = (f32[1,256]{1,0:T(1,128)S(1)}, f32[1,256]{1,0:T(1,128)}, u32[]{:S(2)}) copy-start(f32[1,256]{1,0:T(1,128)} %copy-done.84) | copy-start | bytes 3076
  142.1 130.8 %copy-start.87 = (f32[1,256]{1,0:T(1,128)S(1)}, f32[1,256]{1,0:T(1,128)}, u32[]{:S(2)}) copy-start(f32[1,256]{1,0:T(1,128)} %copy-done.86) | copy-start | bytes 3076
  142.1 130.8 %copy-start.89 = (f32[1,256]{1,0:T(1,128)S(1)}, f32[1,256]{1,0:T(1,128)}, u32[]{:S(2)}) copy-start(f32[1,256]{1,0:T(1,128)} %copy-done.88) | copy-start | bytes 3076
  142.1 130.8 %copy-start.91 = (f32[1,256]{1,0:T(1,128)S(1)}, f32[1,256]{1,0:T(1,128)}, u32[]{:S(2)}) copy-start(f32[1,256]{1,0:T(1,128)} %copy-done.90) | copy-start | bytes 3076
  146.5 263.5 %all-reduce.7.cloned.1.call-start = ((), (), s32[]{:S(2)}) async-start(), calls=%async_computation.1 | async-start | bytes 4194304 | tf_op jit(solution)/shard_map/psum | solution.py:144
  151.2 121.3 %collective-permute-start.6 = (bf16[32,25,256]{2,1,0:T(8,128)(2,1)}, bf16[32,25,256]{2,1,0:T(8,128)(2,1)S(1)}, u32[]{:S(2)}, u32[]{:S(2)}) collective-permute-start(bf16[32,25,256]{2,1,0:T(8,128)(2,1)} %get-tuple-element.117), channel_id=1, source_target_pairs={{1,0},{3,2},{5,4},{7,6},{9,8},{11,10},{13,12},{15,14},{17,16},{19,... | collective-permute-start | bytes 1228808 | tf_op jit(solution)/shard_map/ppermute | solution.py:17
  152.5 120.1 %collective-permute-start.7 = (bf16[32,25,256]{2,1,0:T(8,128)(2,1)S(1)}, bf16[32,25,256]{2,1,0:T(8,128)(2,1)S(1)}, u32[]{:S(2)}, u32[]{:S(2)}) collective-permute-start(bf16[32,25,256]{2,1,0:T(8,128)(2,1)S(1)} %get-tuple-element.118), channel_id=1, source_target_pairs={{0,1},{2,3},{4,5},{6,7},{8,9},{10,11},{12,13},{14,15},{16,17},{18,... | collective-permute-start | bytes 1228808 | tf_op jit(solution)/shard_map/ppermute | solution.py:14
  (69 other events, 1020.4 us)
Sparse Core Ops, SparseCore 0:
  146.6 123.0 all-reduce.4
  275.2 134.7 all-reduce.6
where the time goes:
time: 423 us; the launch traced here: 421 us
  waiting for transfers between devices  244 us (58%)
  other arithmetic  94 us (22%)
  local copies, waits for them, and re-layouts  28.5 us (7%)
  starting transfers between devices  25.2 us (6%)
  between operations  16 us (4%)
  matrix products  13.2 us (3%)
    psum x2, waiting for transfers between devices, local(): lax.psum((sum_in, sum_out, part_wide, part_tall), ('row', 'col'))  237 us
    reduce_sum x5, other arithmetic, correlate_columns(): jnp.sum(gradf * padded[:, offset:offset + length, :].astype(jnp.float32),...  27.9 us
    ppermute x4, starting transfers between devices, with_halo(): lax.ppermute(lax.slice_in_dim(block, block.shape[dim] - width, None, axis...  19.6 us
    reduce_sum x6, other arithmetic, correlate_rows(): jnp.sum(gradf * padded[offset:offset + length].astype(jnp.float32), axis=...  17.3 us
    reduce_sum x1, other arithmetic, mlp_backward(): average = jnp.mean(mixed, axis=-1, keepdims=True)  13.4 us
    convert_element_type x1, other arithmetic, local(): grad_input = (cotangent.astype(jnp.float32) + flip_columns(wide_grad, ker...  12.9 us
    convert_element_type x1, other arithmetic, local(): slide_columns(wide_input, kernel_wide, tile_cols).astype(jnp.bfloat16)  11.3 us
    another operation x1, local copies, waits for them, and re-layouts, correlate_rows(): jnp.stack([jnp.sum(gradf * padded[offset:offset + length].astype(jnp.floa...  9.19 us
  transfers between devices with their start and end apart: 10, of which 4 were waited for; matrix products, arithmetic and copies ran while one was open for 13% of the time, Pallas kernels for 0%

commit v1 on v0

--- a/solution.py
+++ b/solution.py
@@ -1,8 +1,11 @@
+import functools
 import math
 
 import jax
 import jax.numpy as jnp
 from jax import lax
+from jax.experimental import pallas as pl
+from jax.experimental.pallas import tpu as pltpu
 from jax.sharding import PartitionSpec as P
 
 
@@ -99,6 +102,193 @@
     second = jnp.mean(grad_unit * unit, axis=-1, keepdims=True)
     grad_mixed = (rstd_val * (grad_unit - first - unit * second)).astype(jnp.bfloat16)
     return (grad_mixed, sum_in, sum_out)
+
+
+MESH = pl.DeviceIdType.MESH
+
+
+def reduce_kernel(n_row, n_col, factor, big, small, in_out, out_out, small_out, *scratch):
+    nets = []
+    for k, src in enumerate((big, small)):
+        pair_buf, half, slots, cols, whole, s0, r0, s1, r1, s2, r2, s3, r3, s4, r4 = scratch[
+            15 * k : 15 * k + 15
+        ]
+        nets.append((src, pair_buf, half, slots, cols, whole, s0, r0, s1, r1, s2, r2, s3, r3, s4, r4))
+    row, col = lax.axis_index("row"), lax.axis_index("col")
+    m = n_row // 2
+    core, j = lax.rem(row, 2), row // 2
+    pair = (row + 1 - 2 * core, col)
+
+    def peer(d):
+        return (2 * lax.rem(j + d, m) + core, col)
+
+    def col_peer(d):
+        return (row, lax.rem(col + d, n_col))
+
+    def copy(src, dst, send, recv, target):
+        return pltpu.make_async_remote_copy(
+            src_ref=src, dst_ref=dst, send_sem=send, recv_sem=recv, device_id=target, device_id_type=MESH
+        )
+
+    barrier = pltpu.get_barrier_semaphore()
+    pl.semaphore_signal(barrier, inc=1, device_id=pair, device_id_type=MESH)
+
+    @pl.loop(1, m)
+    def _(d):
+        pl.semaphore_signal(barrier, inc=1, device_id=peer(d), device_id_type=MESH)
+
+    @pl.loop(1, n_col)
+    def _(d):
+        pl.semaphore_signal(barrier, inc=1, device_id=col_peer(d), device_id_type=MESH)
+
+    pl.semaphore_wait(barrier, 1 + (m - 1) + (n_col - 1))
+
+    def pair_copy(net):
+        src, pair_buf, s0, r0 = net[0], net[1], net[6], net[7]
+        h = pair_buf.shape[0]
+        other = pl.multiple_of((1 - core) * h, 16)
+        return copy(src.at[pl.ds(other, h)], pair_buf, s0, r0, pair)
+
+    def peer_copy(net, d):
+        half, slots, s1, r1 = net[2], net[3], net[8], net[9]
+        p = slots.shape[1]
+        at = pl.multiple_of(lax.rem(j + d, m) * p, p)
+        return copy(half.at[pl.ds(at, p)], slots.at[d], s1.at[d], r1.at[d], peer(d))
+
+    def col_copy(net, d, c):
+        cols, s2, r2 = net[4], net[10], net[11]
+        return copy(cols.at[c], cols.at[c], s2.at[d], r2.at[c], col_peer(d))
+
+    def back_copy(net, d, owner):
+        slots, whole, s3, r3 = net[3], net[5], net[12], net[13]
+        p = slots.shape[1]
+        at = pl.multiple_of(core * (whole.shape[0] // 2) + owner * p, p)
+        return copy(whole.at[pl.ds(at, p)], whole.at[pl.ds(at, p)], s3.at[d], r3.at[d], peer(d))
+
+    def last_copy(net, side):
+        whole, s4, r4 = net[5], net[14], net[15]
+        h = whole.shape[0] // 2
+        at = pl.multiple_of(side * h, 16)
+        return copy(whole.at[pl.ds(at, h)], whole.at[pl.ds(at, h)], s4, r4, pair)
+
+    for net in nets:
+        pair_copy(net).start()
+    for net in nets:
+        src, pair_buf, half = net[0], net[1], net[2]
+        pair_copy(net).wait()
+        h = half.shape[0]
+        at = pl.multiple_of(core * h, 16)
+        mine = src[pl.ds(at, h), :].astype(jnp.float32)
+        half[...] = (mine + pair_buf[...].astype(jnp.float32)).astype(half.dtype)
+
+        @pl.loop(1, m)
+        def _(d, net=net):
+            peer_copy(net, d).start()
+
+    for net in nets:
+        half, slots, cols = net[2], net[3], net[4]
+        p = slots.shape[1]
+        cols[col] = half[pl.ds(pl.multiple_of(j * p, p), p), :].astype(jnp.float32)
+
+        @pl.loop(1, m)
+        def _(d, net=net, slots=slots, cols=cols):
+            peer_copy(net, d).wait()
+            cols[col] = cols[col] + slots[d].astype(jnp.float32)
+
+        @pl.loop(1, n_col)
+        def _(d, net=net):
+            col_copy(net, d, col).start()
+
+    for net in nets:
+        slots, cols, whole = net[3], net[4], net[5]
+        p = slots.shape[1]
+
+        @pl.loop(1, n_col)
+        def _(d, net=net):
+            col_copy(net, d, col).wait_send()
+            col_copy(net, d, lax.rem(col + d, n_col)).wait_recv()
+
+        total = cols[0]
+        for c in range(1, n_col):
+            total = total + cols[c]
+        at = pl.multiple_of(core * (whole.shape[0] // 2) + j * p, p)
+        whole[pl.ds(at, p), :] = (total * factor).astype(whole.dtype)
+
+        @pl.loop(1, m)
+        def _(d, net=net):
+            back_copy(net, d, j).start()
+
+    for net in nets:
+
+        @pl.loop(1, m)
+        def _(d, net=net):
+            back_copy(net, d, j).wait_send()
+            back_copy(net, d, lax.rem(j + m - d, m)).wait_recv()
+
+        last_copy(net, core).start()
+    for net in nets:
+        last_copy(net, core).wait_send()
+        last_copy(net, 1 - core).wait_recv()
+    whole_big, whole_small = nets[0][5], nets[1][5]
+    depth, wide = in_out.shape
+    blocks = wide // whole_big.shape[1]
+    width = whole_big.shape[1]
+    for b in range(blocks):
+        in_out[:, b * width : (b + 1) * width] = whole_big[b * depth : (b + 1) * depth, :]
+    out_out[...] = whole_big[blocks * depth :, :]
+    small_out[...] = whole_small[...]
+
+
+def reduce_sums(sum_in, sum_out, part_wide, part_tall, factor):
+    n_row, n_col = lax.axis_size("row"), lax.axis_size("col")
+    m = n_row // 2
+    depth, wide = sum_in.shape
+    taps, width = part_wide.shape
+    big = jnp.concatenate(
+        [sum_in[:, b * width : (b + 1) * width] for b in range(wide // width)] + [sum_out], axis=0
+    ).astype(jnp.bfloat16)
+    each = -(-2 * taps // (8 * n_row)) * 8
+    small = jnp.concatenate(
+        [part_wide, part_tall, jnp.zeros((each * n_row - 2 * taps, width), jnp.float32)], axis=0
+    )
+    scratch = []
+    for src in (big, small):
+        rows = src.shape[0]
+        p = rows // n_row
+        dma = pltpu.SemaphoreType.DMA
+        scratch += [
+            pltpu.VMEM((rows // 2, width), src.dtype),
+            pltpu.VMEM((rows // 2, width), src.dtype),
+            pltpu.VMEM((m, p, width), src.dtype),
+            pltpu.VMEM((n_col, p, width), jnp.float32),
+            pltpu.VMEM((rows, width), src.dtype),
+            dma,
+            dma,
+            dma((m,)),
+            dma((m,)),
+            dma((n_col,)),
+            dma((n_col,)),
+            dma((m,)),
+            dma((m,)),
+            dma,
+            dma,
+        ]
+    vmem = pl.BlockSpec(memory_space=pltpu.VMEM)
+    grad_in, grad_out, tapped = pl.pallas_call(
+        functools.partial(reduce_kernel, n_row, n_col, factor),
+        out_shape=(
+            jax.ShapeDtypeStruct(sum_in.shape, jnp.bfloat16),
+            jax.ShapeDtypeStruct(sum_out.shape, jnp.bfloat16),
+            jax.ShapeDtypeStruct(small.shape, jnp.float32),
+        ),
+        in_specs=[vmem] * 2,
+        out_specs=(vmem,) * 3,
+        scratch_shapes=scratch,
+        compiler_params=pltpu.CompilerParams(
+            collective_id=0, has_side_effects=True, vmem_limit_bytes=32 * 1024 * 1024
+        ),
+    )(big, small)
+    return grad_in, grad_out, tapped[:taps], tapped[taps : 2 * taps]
 
 
 def local(
@@ -141,12 +331,10 @@
     part_wide = correlate_columns(grad_hidden, wide_input, taps)
     pixels = tile_rows * lax.axis_size("row") * tile_cols * lax.axis_size("col")
     factor = 1.0 / math.sqrt(pixels)
-    total_in, total_out, total_wide, total_tall = lax.psum(
-        (sum_in, sum_out, part_wide, part_tall), ("row", "col")
-    )
-    grad_in = (total_in * factor).astype(jnp.bfloat16)
-    grad_out = (total_out * factor).astype(jnp.bfloat16)
-    return (grad_input, grad_in, grad_out, total_wide * factor, total_tall * factor)
+    grad_in, grad_out, grad_wide, grad_tall = reduce_sums(
+        sum_in, sum_out, part_wide, part_tall, factor
+    )
+    return (grad_input, grad_in, grad_out, grad_wide, grad_tall)
 
 
 def solution(mesh):

time: 423 us -> 197 us (0.47)
  waiting for transfers between devices: 244 us -> 7.43 us
  Pallas kernels: 0 us -> 40 us
  between operations: 16 us -> 2.67 us
  other arithmetic: 94 us -> 87.5 us
  matrix products: 13.2 us -> 7.54 us
  local copies, waits for them, and re-layouts: 28.5 us -> 24.1 us
    psum x2 -> x0, waiting for transfers between devices: 237 us -> none  [local(): lax.psum((sum_in, sum_out, part_wide, part_tall), ('row', 'col'))]
    pallas_call x0 -> x1, Pallas kernels: none -> 40 us  [reduce_sums(): pl.pallas_call(functools.partial(reduce_kernel, n_row, n_col, factor), ou...]
    another operation x2 -> x0, local copies, waits for them, and re-layouts: 13.5 us -> none  [the longest x1 9.19 us: correlate_rows(): jnp.stack([jnp.sum(gradf * padded[offset:offset + length].astype(jnp.floa...]
    convert_element_type x1, other arithmetic: 12.9 us -> 21.5 us  [local(): grad_input = (cotangent.astype(jnp.float32) + flip_columns(wide_grad, ker...]
    reduce_sum x5, other arithmetic: 27.9 us -> 21.4 us  [correlate_columns(): jnp.sum(gradf * padded[:, offset:offset + length, :].astype(jnp.float32),...]
    concatenate x0 -> x1, local copies, waits for them, and re-layouts: none -> 5.38 us  [reduce_sums(): jnp.concatenate([part_wide, part_tall, jnp.zeros((each * n_row - 2 * taps...]
    convert_element_type x2 -> x0, other arithmetic: 4.23 us -> none  [the longest x1 2.12 us: local(): grad_out = (total_out * factor).astype(jnp.bfloat16)]
  transfers between devices with their start and end apart: 10 -> 8, of which waited for: 4 -> 2; matrix products, arithmetic and copies ran while one was open for 13% -> 17% of each run, Pallas kernels for 0% -> 21%
where the time goes in v1:
time: 197 us; the launch traced here: 195 us
  other arithmetic  87.5 us (44%)
  Pallas kernels  40 us (20%)
  starting transfers between devices  25.7 us (13%)
  local copies, waits for them, and re-layouts  24.1 us (12%)
  matrix products  7.54 us (4%)
  waiting for transfers between devices  7.43 us (4%)
  between operations  2.67 us (1%)
    pallas_call x1, Pallas kernels, reduce_sums(): pl.pallas_call(functools.partial(reduce_kernel, n_row, n_col, factor), ou...  40 us
    convert_element_type x1, other arithmetic, local(): grad_input = (cotangent.astype(jnp.float32) + flip_columns(wide_grad, ker...  21.5 us
    reduce_sum x5, other arithmetic, correlate_columns(): jnp.sum(gradf * padded[:, offset:offset + length, :].astype(jnp.float32),...  21.4 us
    ppermute x4, starting transfers between devices, with_halo(): lax.ppermute(lax.slice_in_dim(block, block.shape[dim] - width, None, axis...  20.4 us
    reduce_sum x6, other arithmetic, correlate_rows(): jnp.sum(gradf * padded[offset:offset + length].astype(jnp.float32), axis=...  16.6 us
    reduce_sum x1, other arithmetic, mlp_backward(): average = jnp.mean(mixed, axis=-1, keepdims=True)  12.6 us
    convert_element_type x1, other arithmetic, local(): slide_columns(wide_input, kernel_wide, tile_cols).astype(jnp.bfloat16)  11.1 us
    ppermute x4, waiting for transfers between devices, with_halo(): lax.ppermute(lax.slice_in_dim(block, 0, width, axis=dim), axis, backward)  7.42 us
  transfers between devices with their start and end apart: 8, of which 2 were waited for; matrix products, arithmetic and copies ran while one was open for 17% of the time, Pallas kernels for 21%

profile of v1, /device:TPU:0, one launch (start us, length us, event | category | flops | bytes accessed | tf_op | source)
XLA Modules:
  0.0 195.0 jit_solution(18232737071981980870)
XLA Ops:
  0.6 0.0 copy-start
  0.6 0.0 copy-start.1
  0.7 1.5 fusion.443
  2.2 4.9 %collective-permute-start = (bf16[32,25,256]{2,1,0:T(8,128)(2,1)S(1)}, bf16[32,25,256]{2,1,0:T(8,128)(2,1)S(1)}, u32[]{:S(2)}, u32[]{:S(2)}) collective-permute-start(bf16[32,25,256]{2,1,0:T(8,128)(2,1)S(1)} %get-tuple-element.125), channel_id=1, source_target_pairs={{0,1},{2,3},{4,5},{6,7},{8,9},{10,11},{12,13},{14,15},{16,17},{18,... | collective-permute-start | bytes 1228808 | tf_op jit(solution)/shard_map/ppermute | solution.py:17
  7.1 1.3 collective-permute-start.1
  8.4 1.0 fusion.448
  9.6 1.0 fusion.449
  10.8 1.7 fusion.445
  12.5 1.6 fusion.450
  14.1 1.1 constant_dynamic-update-slice_fusion.1
  15.1 1.7 fusion.446
  16.8 5.5 %collective-permute-done.1 = bf16[32,25,256]{2,1,0:T(8,128)(2,1)S(1)} collective-permute-done((bf16[32,25,256]{2,1,0:T(8,128)(2,1)S(1)}, bf16[32,25,256]{2,1,0:T(8,128)(2,1)S(1)}, u32[]{:S(2)}, u32[]{:S(2)}) %collective-permute-start.1) | collective-permute-done | bytes 409632 | tf_op jit(solution)/shard_map/ppermute | solution.py:20
  22.8 0.0 copy-start.113
  22.8 11.1 %fusion.264 = bf16[32,32,256]{2,1,0:T(8,128)(2,1)S(1)} fusion(bf16[32,32,256]{2,1,0:T(8,128)(2,1)S(1)} %copy-done.1, f32[256]{0:T(256)} %bitcast.51, f32[256]{0:T(256)} %bitcast.50, f32[256]{0:T(256)S(1)} %bitcast.287, f32[256]{0:T(256)S(1)} %bitcast.289, f32[256]{0:T(256)S(1)} %bitcast.291, f32[256]{0:T(256)S(1)} %bitcast.293, f32[256]{0:T(256)S(1)} %bitcast.295, ...), kind=kLoop, calls=%fused_computation.819 | loop fusion | flops 59768832 | bytes 14617600 | tf_op jit(solution)/shard_map/convert_element_type | solution.py:310
  34.0 0.1 fusion.442
  34.1 1.3 collective-permute-start.2
  35.4 1.5 collective-permute-start.3
  36.9 0.9 fusion.447
  38.0 0.9 fusion.263
  38.9 1.9 collective-permute-done.3
  40.8 0.7 copy-done.5
  41.5 12.6 %fusion.438 = (f32[32,32]{1,0:T(8,128)S(1)}, f32[32,32,256]{2,1,0:T(8,128)S(1)}) fusion(bf16[25,32,256]{2,1,0:T(8,128)(2,1)S(1)} %collective-permute-done.3, bf16[32,32,256]{2,1,0:T(8,128)(2,1)S(1)} %fusion.264, f32[256]{0:T(256)S(1)} %bitcast.383, f32[256]{0:T(256)S(1)} %bitcast.385, f32[256]{0:T(256)} %bitcast.99, f32[256]{0:T(256)} %bitcast.98, ...), kind=kLoop, calls=%fused_computation.1010 | loop fusion | flops 53214208 | bytes 2448384 | tf_op jit(solution)/shard_map/reduce_sum | solution.py:86
  54.3 0.6 broadcast_multiply_fusion
  54.9 1.4 div.16
  56.2 1.1 multiply_reduce_fusion.1
  57.3 0.6 add_rsqrt_fusion
  58.0 1.4 rsqrt.12
  59.3 1.1 add_convert_fusion.2
  60.4 0.0 copy-start.9
  60.4 0.0 copy-start.115
  60.5 0.7 fusion.451
  61.2 0.3 copy-done.9
  61.5 0.2 copy-done.115
  61.6 3.3 %fusion.6 = bf16[1024,1024]{1,0:T(8,128)(2,1)S(1)} fusion(f32[1024,1024]{1,0:T(8,128)S(1)} %fusion.451, bf16[1024,256]{1,0:T(8,128)(2,1)S(1)} %copy-done.9, bf16[1024,256]{1,0:T(8,128)(2,1)S(1)} %copy-done.115, f32[1024]{0:T(1024)S(1)} %copy-done.116), kind=kOutput, calls=%fused_computation.352 | convolution fusion | flops 558891008 | bytes 7344128 | tf_op jit(solution)/shard_map/dot_general | solution.py:97
  64.9 0.0 copy-start.6
  64.9 0.7 convolution_convert_fusion
  65.7 0.9 fusion.437
  66.6 7.3 %fusion.184 = (f32[256]{0:T(256)}, f32[256]{0:T(256)}, f32[256]{0:T(256)}, f32[256]{0:T(256)}, f32[256]{0:T(256)}, /*index=5*/f32[256]{0:T(256)}, f32[256]{0:T(2...) fusion(bf16[25,32,256]{2,1,0:T(8,128)(2,1)S(1)} %copy-done.6, bf16[32,32,256]{2,1,0:T(8,128)(2,1)S(1)} %fusion.264, ...), kind=kLoop, calls=%fused_computation.731 | loop fusion | flops 11532032 | bytes 3580928 | tf_op jit(solution)/shard_map/reduce_sum | solution.py:75
  74.0 0.1 fusion.441
  74.0 8.1 %collective-permute-start.5 = (bf16[25,32,256]{2,1,0:T(8,128)(2,1)S(1)}, bf16[25,32,256]{2,1,0:T(8,128)(2,1)S(1)}, u32[]{:S(2)}, u32[]{:S(2)}) collective-permute-start(bf16[25,32,256]{2,1,0:T(8,128)(2,1)S(1)} %bitcast.284), channel_id=1, source_target_pairs={{0,2},{2,4},{4,6},{6,8},{8,10},{10,12},{12,14},{14,16},{16,18},{18... | collective-permute-start | bytes 1228808 | tf_op jit(solution)/shard_map/ppermute | solution.py:17
  82.1 1.3 collective-permute-start.4
  83.5 1.9 fusion.9.big
  85.6 1.8 fusion.175
  87.4 1.9 fusion.185
  89.3 1.9 fusion.159
  91.3 1.9 fusion.158
  93.2 1.7 fusion.149
  95.0 12.9 %fusion.260 = (f32[256]{0:T(256)S(1)}, f32[256]{0:T(256)S(1)}, f32[256]{0:T(256)S(1)}, f32[256]{0:T(256)S(1)}, f32[256]{0:T(256)S(1)}, /*index=5*/f32[256]{0:T(2...) fusion(bf16[32,57,256]{2,1,0:T(8,128)(2,1)S(1)} %constant_dynamic-update-slice_fusion, ...), kind=kLoop, calls=%fused_computation.807 | loop fusion | flops 58980608 | bytes 5597184 | tf_op jit(solution)/shard_map/reduce_sum | solution.py:64
  107.9 0.0 copy-start.2
  107.9 0.0 copy-start.4
  107.9 2.7 %fusion.261 = (f32[256]{0:T(256)S(1)}, f32[256]{0:T(256)S(1)}, f32[256]{0:T(256)S(1)}, f32[256]{0:T(256)S(1)}, f32[256]{0:T(256)S(1)}, /*index=5*/f32[256]{0:T(2...) fusion(bf16[32,32,256]{2,1,0:T(8,128)(2,1)S(1)} %get-tuple-elem, ...), kind=kLoop, calls=%fused_computation.808 | loop fusion | flops 14413312 | bytes 9979904 | tf_op jit(solution)/shard_map/reduce_sum | solution.py:64
  110.7 0.0 copy-start.8
  111.1 1.3 fusion.440
  112.3 1.3 collective-permute-start.6
  113.6 6.1 %collective-permute-start.7 = (bf16[32,25,256]{2,1,0:T(8,128)(2,1)}, bf16[32,25,256]{2,1,0:T(8,128)(2,1)}, u32[]{:S(2)}, u32[]{:S(2)}) collective-permute-start(bf16[32,25,256]{2,1,0:T(8,128)(2,1)} %get-tuple-element.120), channel_id=1, source_target_pairs={{0,1},{2,3},{4,5},{6,7},{8,9},{10,11},{12,13},{14,15},{16,17},{18,... | collective-permute-start | bytes 1228808 | tf_op jit(solution)/shard_map/ppermute | solution.py:17
  119.8 2.2 %fusion.235 = (f32[256]{0:T(256)S(1)}, f32[256]{0:T(256)S(1)}, f32[256]{0:T(256)S(1)}, f32[256]{0:T(256)S(1)}, f32[256]{0:T(256)S(1)}, /*index=5*/f32[256]{0:T(2...) fusion(bf16[32,32,256]{2,1,0:T(8,128)(2,1)S(1)} %get-tuple-element.116, bf16[32,32,256]{2,1,0:T(8,128)(2,1)S(1)} %copy-done.2, ...), kind=kLoop, calls=%fused_computation.782 | loop fusion | flops 14415616 | bytes 1467392 | tf_op jit(solution)/shard_map/reduce_sum | solution.py:64
  122.0 1.9 fusion.234
  123.8 1.6 fusion.233
  125.5 5.4 %concatenate.236.small = f32[128,256]{1,0:T(8,128)S(1)} concatenate(f32[1,256]{1,0:T(1,128)S(1)} %bitcast.434, f32[1,256]{1,0:T(1,128)S(1)} %bitcast.433, f32[1,256]{1,0:T(1,128)S(1)} %bitcast.431, f32[1,256]{1,0:T(1,128)S(1)} %bitcast.432, f32[1,256]{1,0:T(1,128)S(1)} %bitcast.445, f32[1,256]{1,0:T(1,128)S(1)} %bitcast.446, f32[1,256]{1,0:T(1,128)S(1)} %bitcast.447, ...), dimensions={0} | concatenate | bytes 262144 | tf_op jit(solution)/shard_map/concatenate | solution.py:251
  130.9 40.0 %shard_map.137 = (bf16[256,1024]{1,0:T(8,128)(2,1)S(1)}, bf16[1024,256]{1,0:T(8,128)(2,1)S(1)}, f32[128,256]{1,0:T(8,128)S(1)}) custom-call(bf16[2048,256]{1,0:T(8,128)(2,1)S(1)} %fusion.9.big, f32[128,256]{1,0:T(8,128)S(1)} %concatenate.236.small), custom_call_target="tpu_custom_call" | custom-call | tf_op jit(solution)/shard_map/pallas_call | solution.py:277
  170.9 0.7 fusion.444
  171.9 21.5 %add_convert_fusion = bf16[32,32,256]{2,1,0:T(8,128)(2,1)} fusion(bf16[32,32,256]{2,1,0:T(8,128)(2,1)S(1)} %get-tuple-element.116, bf16[32,25,256]{2,1,0:T(8,128)(2,1)} %collective-permute-done.7, bf16[32,25,256]{2,1,0:T(8,128)(2,1)} %collective-permute-done.6, f32[256]{0:T(256)} %bitcast.51, f32[256]{0:T(256)} %bitcast.50, f32[256]{0:T(256)S(1)} %bitcast.288, ...), kind=kLoop, calls=%fused_computation.813 | loop fusion | flops 79953920 | bytes 2444288 | tf_op jit(solution)/shard_map/convert_element_type | solution.py:329
  193.4 0.8 copy.22
  194.2 0.8 copy.23
  (235 shorter events, 0.6 us)
Async XLA Ops:
  0.6 59.8 %copy-start = (bf16[256,1024]{1,0:T(8,128)(2,1)S(1)}, bf16[256,1024]{1,0:T(8,128)(2,1)}, u32[]{:S(2)}) copy-start(bf16[256,1024]{1,0:T(8,128)(2,1)} %param.16) | copy-start | bytes 1572868
  0.6 22.1 %copy-start.1 = (bf16[32,32,256]{2,1,0:T(8,128)(2,1)S(1)}, bf16[32,32,256]{2,1,0:T(8,128)(2,1)}, u32[]{:S(2)}) copy-start(bf16[32,32,256]{2,1,0:T(8,128)(2,1)} %param.10) | copy-start | bytes 1572868
  2.2 20.2 %collective-permute-start = (bf16[32,25,256]{2,1,0:T(8,128)(2,1)S(1)}, bf16[32,25,256]{2,1,0:T(8,128)(2,1)S(1)}, u32[]{:S(2)}, u32[]{:S(2)}) collective-permute-start(bf16[32,25,256]{2,1,0:T(8,128)(2,1)S(1)} %get-tuple-element.125), channel_id=1, source_target_pairs={{0,1},{2,3},{4,5},{6,7},{8,9},{10,11},{12,13},{14,15},{16,17},{18,... | collective-permute-start | bytes 1228808 | tf_op jit(solution)/shard_map/ppermute | solution.py:17
  7.1 15.3 %collective-permute-start.1 = (bf16[32,25,256]{2,1,0:T(8,128)(2,1)S(1)}, bf16[32,25,256]{2,1,0:T(8,128)(2,1)S(1)}, u32[]{:S(2)}, u32[]{:S(2)}) collective-permute-start(bf16[32,25,256]{2,1,0:T(8,128)(2,1)S(1)} %get-tuple-element.126), channel_id=1, source_target_pairs={{1,0},{3,2},{5,4},{7,6},{9,8},{11,10},{13,12},{15,14},{17,16},{19,... | collective-permute-start | bytes 1228808 | tf_op jit(solution)/shard_map/ppermute | solution.py:20
  9.4 13.0 %copy-start.12 = (f32[1,256]{1,0:T(1,128)}, f32[1,256]{1,0:T(1,128)S(1)}, u32[]{:S(2)}) copy-start(f32[1,256]{1,0:T(1,128)S(1)} %get-tuple-element.180) | copy-start | bytes 3076
  22.8 15.0 %copy-start.7 = (bf16[32,32,256]{2,1,0:T(8,128)(2,1)S(1)}, bf16[32,32,256]{2,1,0:T(8,128)(2,1)}, u32[]{:S(2)}) copy-start(bf16[32,32,256]{2,1,0:T(8,128)(2,1)} %param.11) | copy-start | bytes 1572868
  22.8 15.0 %copy-start.113 = (f32[256]{0:T(256)S(1)}, f32[256]{0:T(256)}, u32[]{:S(2)}) copy-start(f32[256]{0:T(256)} %param.19) | copy-start | bytes 3076
  34.1 4.8 %collective-permute-start.2 = (bf16[25,32,256]{2,1,0:T(8,128)(2,1)S(1)}, bf16[25,32,256]{2,1,0:T(8,128)(2,1)S(1)}, u32[]{:S(2)}, u32[]{:S(2)}) collective-permute-start(bf16[25,32,256]{2,1,0:T(8,128)(2,1)S(1)} %get-tuple-element.123), channel_id=1, source_target_pairs={{0,2},{2,4},{4,6},{6,8},{8,10},{10,12},{12,14},{14,16},{16,18},{18... | collective-permute-start | bytes 1228808 | tf_op jit(solution)/shard_map/ppermute | solution.py:17
  35.4 5.4 %collective-permute-start.3 = (bf16[25,32,256]{2,1,0:T(8,128)(2,1)S(1)}, bf16[25,32,256]{2,1,0:T(8,128)(2,1)S(1)}, u32[]{:S(2)}, u32[]{:S(2)}) collective-permute-start(bf16[25,32,256]{2,1,0:T(8,128)(2,1)S(1)} %get-tuple-element.124), channel_id=1, source_target_pairs={{2,0},{4,2},{6,4},{8,6},{10,8},{12,10},{14,12},{16,14},{18,16},{20... | collective-permute-start | bytes 1228808 | tf_op jit(solution)/shard_map/ppermute | solution.py:20
  37.9 16.3 %copy-start.87 = (f32[1,256]{1,0:T(1,128)}, f32[1,256]{1,0:T(1,128)S(1)}, u32[]{:S(2)}) copy-start(f32[1,256]{1,0:T(1,128)S(1)} %get-tuple-element.167) | copy-start | bytes 3076
  37.9 16.3 %copy-start.89 = (f32[1,256]{1,0:T(1,128)}, f32[1,256]{1,0:T(1,128)S(1)}, u32[]{:S(2)}) copy-start(f32[1,256]{1,0:T(1,128)S(1)} %get-tuple-element.168) | copy-start | bytes 3076
  37.9 16.3 %copy-start.91 = (f32[1,256]{1,0:T(1,128)}, f32[1,256]{1,0:T(1,128)S(1)}, u32[]{:S(2)}) copy-start(f32[1,256]{1,0:T(1,128)S(1)} %get-tuple-element.169) | copy-start | bytes 3076
  37.9 16.3 %copy-start.93 = (f32[1,256]{1,0:T(1,128)}, f32[1,256]{1,0:T(1,128)S(1)}, u32[]{:S(2)}) copy-start(f32[1,256]{1,0:T(1,128)S(1)} %get-tuple-element.170) | copy-start | bytes 3076
  37.9 16.3 %copy-start.95 = (f32[1,256]{1,0:T(1,128)}, f32[1,256]{1,0:T(1,128)S(1)}, u32[]{:S(2)}) copy-start(f32[1,256]{1,0:T(1,128)S(1)} %get-tuple-element.171) | copy-start | bytes 3076
  37.9 16.3 %copy-start.97 = (f32[1,256]{1,0:T(1,128)}, f32[1,256]{1,0:T(1,128)S(1)}, u32[]{:S(2)}) copy-start(f32[1,256]{1,0:T(1,128)S(1)} %get-tuple-element.172) | copy-start | bytes 3076
  37.9 16.3 %copy-start.99 = (f32[1,256]{1,0:T(1,128)}, f32[1,256]{1,0:T(1,128)S(1)}, u32[]{:S(2)}) copy-start(f32[1,256]{1,0:T(1,128)S(1)} %get-tuple-element.173) | copy-start | bytes 3076
  37.9 16.3 %copy-start.101 = (f32[1,256]{1,0:T(1,128)}, f32[1,256]{1,0:T(1,128)S(1)}, u32[]{:S(2)}) copy-start(f32[1,256]{1,0:T(1,128)S(1)} %get-tuple-element.174) | copy-start | bytes 3076
  37.9 16.3 %copy-start.103 = (f32[1,256]{1,0:T(1,128)}, f32[1,256]{1,0:T(1,128)S(1)}, u32[]{:S(2)}) copy-start(f32[1,256]{1,0:T(1,128)S(1)} %get-tuple-element.175) | copy-start | bytes 3076
  37.9 16.3 %copy-start.105 = (f32[1,256]{1,0:T(1,128)}, f32[1,256]{1,0:T(1,128)S(1)}, u32[]{:S(2)}) copy-start(f32[1,256]{1,0:T(1,128)S(1)} %get-tuple-element.176) | copy-start | bytes 3076
  38.0 16.3 %copy-start.107 = (f32[1,256]{1,0:T(1,128)}, f32[1,256]{1,0:T(1,128)S(1)}, u32[]{:S(2)}) copy-start(f32[1,256]{1,0:T(1,128)S(1)} %get-tuple-element.177) | copy-start | bytes 3076
  38.0 16.3 %copy-start.109 = (f32[1,256]{1,0:T(1,128)}, f32[1,256]{1,0:T(1,128)S(1)}, u32[]{:S(2)}) copy-start(f32[1,256]{1,0:T(1,128)S(1)} %get-tuple-element.178) | copy-start | bytes 3076
  38.0 16.3 %copy-start.111 = (f32[1,256]{1,0:T(1,128)}, f32[1,256]{1,0:T(1,128)S(1)}, u32[]{:S(2)}) copy-start(f32[1,256]{1,0:T(1,128)S(1)} %get-tuple-element.179) | copy-start | bytes 3076
  74.0 20.8 %collective-permute-start.5 = (bf16[25,32,256]{2,1,0:T(8,128)(2,1)S(1)}, bf16[25,32,256]{2,1,0:T(8,128)(2,1)S(1)}, u32[]{:S(2)}, u32[]{:S(2)}) collective-permute-start(bf16[25,32,256]{2,1,0:T(8,128)(2,1)S(1)} %bitcast.284), channel_id=1, source_target_pairs={{0,2},{2,4},{4,6},{6,8},{8,10},{10,12},{12,14},{14,16},{16,18},{18... | collective-permute-start | bytes 1228808 | tf_op jit(solution)/shard_map/ppermute | solution.py:17
  82.1 12.8 %collective-permute-start.4 = (bf16[25,32,256]{2,1,0:T(8,128)(2,1)S(1)}, bf16[25,32,256]{2,1,0:T(8,128)(2,1)S(1)}, u32[]{:S(2)}, u32[]{:S(2)}) collective-permute-start(bf16[25,32,256]{2,1,0:T(8,128)(2,1)S(1)} %bitcast.283), channel_id=1, source_target_pairs={{2,0},{4,2},{6,4},{8,6},{10,8},{12,10},{14,12},{16,14},{18,16},{20... | collective-permute-start | bytes 1228808 | tf_op jit(solution)/shard_map/ppermute | solution.py:20
  110.7 60.9 %copy-start.8 = (bf16[32,32,256]{2,1,0:T(8,128)(2,1)S(1)}, bf16[32,32,256]{2,1,0:T(8,128)(2,1)}, u32[]{:S(2)}) copy-start(bf16[32,32,256]{2,1,0:T(8,128)(2,1)} %param.11) | copy-start | bytes 1572868
  110.7 60.8 %copy-start.13 = (f32[1,256]{1,0:T(1,128)S(1)}, f32[1,256]{1,0:T(1,128)}, u32[]{:S(2)}) copy-start(f32[1,256]{1,0:T(1,128)} %copy-done.12) | copy-start | bytes 3076
  110.7 60.8 %copy-start.15 = (f32[1,256]{1,0:T(1,128)S(1)}, f32[1,256]{1,0:T(1,128)}, u32[]{:S(2)}) copy-start(f32[1,256]{1,0:T(1,128)} %copy-done.14) | copy-start | bytes 3076
  110.7 60.8 %copy-start.17 = (f32[1,256]{1,0:T(1,128)S(1)}, f32[1,256]{1,0:T(1,128)}, u32[]{:S(2)}) copy-start(f32[1,256]{1,0:T(1,128)} %copy-done.16) | copy-start | bytes 3076
  110.7 60.8 %copy-start.19 = (f32[1,256]{1,0:T(1,128)S(1)}, f32[1,256]{1,0:T(1,128)}, u32[]{:S(2)}) copy-start(f32[1,256]{1,0:T(1,128)} %copy-done.18) | copy-start | bytes 3076
  110.7 60.8 %copy-start.21 = (f32[1,256]{1,0:T(1,128)S(1)}, f32[1,256]{1,0:T(1,128)}, u32[]{:S(2)}) copy-start(f32[1,256]{1,0:T(1,128)} %copy-done.20) | copy-start | bytes 3076
  110.7 60.8 %copy-start.23 = (f32[1,256]{1,0:T(1,128)S(1)}, f32[1,256]{1,0:T(1,128)}, u32[]{:S(2)}) copy-start(f32[1,256]{1,0:T(1,128)} %copy-done.22) | copy-start | bytes 3076
  110.7 60.8 %copy-start.25 = (f32[1,256]{1,0:T(1,128)S(1)}, f32[1,256]{1,0:T(1,128)}, u32[]{:S(2)}) copy-start(f32[1,256]{1,0:T(1,128)} %copy-done.24) | copy-start | bytes 3076
  110.8 60.8 %copy-start.27 = (f32[1,256]{1,0:T(1,128)S(1)}, f32[1,256]{1,0:T(1,128)}, u32[]{:S(2)}) copy-start(f32[1,256]{1,0:T(1,128)} %copy-done.26) | copy-start | bytes 3076
  110.8 60.8 %copy-start.29 = (f32[1,256]{1,0:T(1,128)S(1)}, f32[1,256]{1,0:T(1,128)}, u32[]{:S(2)}) copy-start(f32[1,256]{1,0:T(1,128)} %copy-done.28) | copy-start | bytes 3076
  110.8 60.8 %copy-start.31 = (f32[1,256]{1,0:T(1,128)S(1)}, f32[1,256]{1,0:T(1,128)}, u32[]{:S(2)}) copy-start(f32[1,256]{1,0:T(1,128)} %copy-done.30) | copy-start | bytes 3076
  110.8 60.8 %copy-start.33 = (f32[1,256]{1,0:T(1,128)S(1)}, f32[1,256]{1,0:T(1,128)}, u32[]{:S(2)}) copy-start(f32[1,256]{1,0:T(1,128)} %copy-done.32) | copy-start | bytes 3076
  110.8 60.8 %copy-start.35 = (f32[1,256]{1,0:T(1,128)S(1)}, f32[1,256]{1,0:T(1,128)}, u32[]{:S(2)}) copy-start(f32[1,256]{1,0:T(1,128)} %copy-done.34) | copy-start | bytes 3076
  110.8 60.8 %copy-start.37 = (f32[1,256]{1,0:T(1,128)S(1)}, f32[1,256]{1,0:T(1,128)}, u32[]{:S(2)}) copy-start(f32[1,256]{1,0:T(1,128)} %copy-done.36) | copy-start | bytes 3076
  110.8 60.8 %copy-start.39 = (f32[1,256]{1,0:T(1,128)S(1)}, f32[1,256]{1,0:T(1,128)}, u32[]{:S(2)}) copy-start(f32[1,256]{1,0:T(1,128)} %copy-done.38) | copy-start | bytes 3076
  110.8 60.8 %copy-start.41 = (f32[1,256]{1,0:T(1,128)S(1)}, f32[1,256]{1,0:T(1,128)}, u32[]{:S(2)}) copy-start(f32[1,256]{1,0:T(1,128)} %copy-done.40) | copy-start | bytes 3076
  110.8 60.8 %copy-start.43 = (f32[1,256]{1,0:T(1,128)S(1)}, f32[1,256]{1,0:T(1,128)}, u32[]{:S(2)}) copy-start(f32[1,256]{1,0:T(1,128)} %copy-done.42) | copy-start | bytes 3076
  110.8 60.8 %copy-start.45 = (f32[1,256]{1,0:T(1,128)S(1)}, f32[1,256]{1,0:T(1,128)}, u32[]{:S(2)}) copy-start(f32[1,256]{1,0:T(1,128)} %copy-done.44) | copy-start | bytes 3076
  110.9 60.8 %copy-start.47 = (f32[1,256]{1,0:T(1,128)S(1)}, f32[1,256]{1,0:T(1,128)}, u32[]{:S(2)}) copy-start(f32[1,256]{1,0:T(1,128)} %copy-done.46) | copy-start | bytes 3076
  110.9 60.8 %copy-start.49 = (f32[1,256]{1,0:T(1,128)S(1)}, f32[1,256]{1,0:T(1,128)}, u32[]{:S(2)}) copy-start(f32[1,256]{1,0:T(1,128)} %copy-done.48) | copy-start | bytes 3076
  110.9 60.8 %copy-start.51 = (f32[1,256]{1,0:T(1,128)S(1)}, f32[1,256]{1,0:T(1,128)}, u32[]{:S(2)}) copy-start(f32[1,256]{1,0:T(1,128)} %copy-done.50) | copy-start | bytes 3076
  110.9 60.8 %copy-start.53 = (f32[1,256]{1,0:T(1,128)S(1)}, f32[1,256]{1,0:T(1,128)}, u32[]{:S(2)}) copy-start(f32[1,256]{1,0:T(1,128)} %copy-done.52) | copy-start | bytes 3076
  110.9 60.8 %copy-start.55 = (f32[1,256]{1,0:T(1,128)S(1)}, f32[1,256]{1,0:T(1,128)}, u32[]{:S(2)}) copy-start(f32[1,256]{1,0:T(1,128)} %copy-done.54) | copy-start | bytes 3076
  110.9 60.8 %copy-start.57 = (f32[1,256]{1,0:T(1,128)S(1)}, f32[1,256]{1,0:T(1,128)}, u32[]{:S(2)}) copy-start(f32[1,256]{1,0:T(1,128)} %copy-done.56) | copy-start | bytes 3076
  110.9 60.8 %copy-start.59 = (f32[1,256]{1,0:T(1,128)S(1)}, f32[1,256]{1,0:T(1,128)}, u32[]{:S(2)}) copy-start(f32[1,256]{1,0:T(1,128)} %copy-done.58) | copy-start | bytes 3076
  110.9 60.8 %copy-start.61 = (f32[1,256]{1,0:T(1,128)S(1)}, f32[1,256]{1,0:T(1,128)}, u32[]{:S(2)}) copy-start(f32[1,256]{1,0:T(1,128)} %copy-done.60) | copy-start | bytes 3076
  110.9 60.8 %copy-start.63 = (f32[1,256]{1,0:T(1,128)S(1)}, f32[1,256]{1,0:T(1,128)}, u32[]{:S(2)}) copy-start(f32[1,256]{1,0:T(1,128)} %copy-done.62) | copy-start | bytes 3076
  110.9 60.8 %copy-start.65 = (f32[1,256]{1,0:T(1,128)S(1)}, f32[1,256]{1,0:T(1,128)}, u32[]{:S(2)}) copy-start(f32[1,256]{1,0:T(1,128)} %copy-done.64) | copy-start | bytes 3076
  111.0 60.8 %copy-start.67 = (f32[1,256]{1,0:T(1,128)S(1)}, f32[1,256]{1,0:T(1,128)}, u32[]{:S(2)}) copy-start(f32[1,256]{1,0:T(1,128)} %copy-done.66) | copy-start | bytes 3076
  111.0 60.8 %copy-start.69 = (f32[1,256]{1,0:T(1,128)S(1)}, f32[1,256]{1,0:T(1,128)}, u32[]{:S(2)}) copy-start(f32[1,256]{1,0:T(1,128)} %copy-done.68) | copy-start | bytes 3076
  111.0 60.8 %copy-start.71 = (f32[1,256]{1,0:T(1,128)S(1)}, f32[1,256]{1,0:T(1,128)}, u32[]{:S(2)}) copy-start(f32[1,256]{1,0:T(1,128)} %copy-done.70) | copy-start | bytes 3076
  111.0 60.8 %copy-start.73 = (f32[1,256]{1,0:T(1,128)S(1)}, f32[1,256]{1,0:T(1,128)}, u32[]{:S(2)}) copy-start(f32[1,256]{1,0:T(1,128)} %copy-done.72) | copy-start | bytes 3076
  111.0 60.8 %copy-start.75 = (f32[1,256]{1,0:T(1,128)S(1)}, f32[1,256]{1,0:T(1,128)}, u32[]{:S(2)}) copy-start(f32[1,256]{1,0:T(1,128)} %copy-done.74) | copy-start | bytes 3076
  111.0 60.8 %copy-start.77 = (f32[1,256]{1,0:T(1,128)S(1)}, f32[1,256]{1,0:T(1,128)}, u32[]{:S(2)}) copy-start(f32[1,256]{1,0:T(1,128)} %copy-done.76) | copy-start | bytes 3076
  111.0 60.8 %copy-start.79 = (f32[1,256]{1,0:T(1,128)S(1)}, f32[1,256]{1,0:T(1,128)}, u32[]{:S(2)}) copy-start(f32[1,256]{1,0:T(1,128)} %copy-done.78) | copy-start | bytes 3076
  111.0 60.8 %copy-start.81 = (f32[1,256]{1,0:T(1,128)S(1)}, f32[1,256]{1,0:T(1,128)}, u32[]{:S(2)}) copy-start(f32[1,256]{1,0:T(1,128)} %copy-done.80) | copy-start | bytes 3076
  111.0 60.8 %copy-start.83 = (f32[1,256]{1,0:T(1,128)S(1)}, f32[1,256]{1,0:T(1,128)}, u32[]{:S(2)}) copy-start(f32[1,256]{1,0:T(1,128)} %copy-done.82) | copy-start | bytes 3076
  111.0 60.8 %copy-start.85 = (f32[1,256]{1,0:T(1,128)S(1)}, f32[1,256]{1,0:T(1,128)}, u32[]{:S(2)}) copy-start(f32[1,256]{1,0:T(1,128)} %copy-done.84) | copy-start | bytes 3076
  112.3 59.2 %collective-permute-start.6 = (bf16[32,25,256]{2,1,0:T(8,128)(2,1)}, bf16[32,25,256]{2,1,0:T(8,128)(2,1)}, u32[]{:S(2)}, u32[]{:S(2)}) collective-permute-start(bf16[32,25,256]{2,1,0:T(8,128)(2,1)} %get-tuple-element.119), channel_id=1, source_target_pairs={{1,0},{3,2},{5,4},{7,6},{9,8},{11,10},{13,12},{15,14},{17,16},{19,... | collective-permute-start | bytes 1228808 | tf_op jit(solution)/shard_map/ppermute | solution.py:20
  113.6 57.9 %collective-permute-start.7 = (bf16[32,25,256]{2,1,0:T(8,128)(2,1)}, bf16[32,25,256]{2,1,0:T(8,128)(2,1)}, u32[]{:S(2)}, u32[]{:S(2)}) collective-permute-start(bf16[32,25,256]{2,1,0:T(8,128)(2,1)} %get-tuple-element.120), channel_id=1, source_target_pairs={{0,1},{2,3},{4,5},{6,7},{8,9},{10,11},{12,13},{14,15},{16,17},{18,... | collective-permute-start | bytes 1228808 | tf_op jit(solution)/shard_map/ppermute | solution.py:17
  (61 other events, 638.0 us)

commit v2 on v0

v2 whole, which is shorter than its diff:
```python
import functools
import math

import jax
import jax.numpy as jnp
from jax import lax
from jax.experimental import pallas as pl
from jax.experimental.pallas import tpu as pltpu
from jax.sharding import PartitionSpec as P


def gelu_tanh(value):
    return jax.nn.gelu(value, approximate=True)


def mlp_backward(mixed, cot, norm_gain, norm_bias, weight_in, bias_in, weight_out, layer_scale):
    average = jnp.mean(mixed, axis=-1, keepdims=True)
    centred = mixed - average
    spread = jnp.mean(centred * centred, axis=-1, keepdims=True)
    rstd_val = lax.rsqrt(spread + 1e-06)
    unit = centred * rstd_val
    normed = (unit * norm_gain + norm_bias).astype(jnp.bfloat16)
    pre = jnp.dot(normed, weight_in, preferred_element_type=jnp.float32) + bias_in
    lifted_f, pullback = jax.vjp(gelu_tanh, pre)
    lifted = lifted_f.astype(jnp.bfloat16)
    scaled_cot = (layer_scale * cot.astype(jnp.float32)).astype(jnp.bfloat16)
    sum_out = jnp.dot(lifted.T, scaled_cot, preferred_element_type=jnp.float32)
    grad_lift = jnp.dot(scaled_cot, weight_out.T, preferred_element_type=jnp.float32)
    grad_pre = pullback(grad_lift)[0].astype(jnp.bfloat16)
    sum_in = jnp.dot(normed.T, grad_pre, preferred_element_type=jnp.float32)
    grad_unit = jnp.dot(grad_pre, weight_in.T, preferred_element_type=jnp.float32) * norm_gain
    first = jnp.mean(grad_unit, axis=-1, keepdims=True)
    second = jnp.mean(grad_unit * unit, axis=-1, keepdims=True)
    grad_mixed = (rstd_val * (grad_unit - first - unit * second)).astype(jnp.bfloat16)
    return (grad_mixed, sum_in, sum_out)


MESH = pl.DeviceIdType.MESH
GROUP = 8
LANES = 128


def remote(src, dst, send, recv, target):
    return pltpu.make_async_remote_copy(
        src_ref=src, dst_ref=dst, send_sem=send, recv_sem=recv, device_id=target, device_id_type=MESH
    )


def below(at, count):
    return (at + count - 1) // count


def above(at, count):
    return (2 * count - 2 - at) // count


def greet(barrier, target):
    pl.semaphore_signal(barrier, inc=1, device_id=target, device_id_type=MESH)


def taps_loop(acc, lo, hi, one, unroll=5):
    steps = max(hi - lo, 0) // unroll

    def body(s, acc):
        for u in range(unroll):
            acc = one(lo + s * unroll + u, acc)
        return acc

    if steps > 0:
        acc = lax.fori_loop(0, steps, body, acc)
    for o in range(lo + steps * unroll, hi):
        acc = one(o, acc)
    return acc


def conv_pass(padded, kernel, flip, minor, ranges, blocks, start, finish):
    last = kernel.shape[0] // 8 - 1
    size = GROUP * minor
    for b in blocks:

        @pl.loop(0, padded.shape[0])
        def _(part, b=b):
            lane = pl.ds(pl.multiple_of(part * LANES, LANES), LANES)

            def one(o, acc):
                tap_at = (last - o if flip else o) * 8
                tap_at = tap_at if isinstance(tap_at, int) else pl.multiple_of(tap_at, 8)
                tap = kernel[pl.ds(tap_at, 8), lane]
                at = b * size + o * minor
                at = at if isinstance(at, int) else pl.multiple_of(at, 8)
                return acc + tap[None] * padded[part, pl.ds(at, size), :].reshape(size // 8, 8, LANES)

            acc = start(b, lane).reshape(size // 8, 8, LANES)
            for lo, hi in ranges(b):
                acc = taps_loop(acc, lo, hi, one)
            finish(b, part, lane, acc.reshape(size, LANES))


def correlate(grad_at, grad, padded, taps, minor, sums, out, out_at):
    lead = (padded.shape[1] // minor) - taps + 1
    size = GROUP * minor
    for b in range(lead // GROUP):

        @pl.loop(0, padded.shape[0])
        def _(part, b=b):
            lane = pl.ds(pl.multiple_of(part * LANES, LANES), LANES)
            own = grad[part, pl.ds(grad_at + b * size, size), :]

            def one(o, carry):
                at = b * size + o * minor
                at = at if isinstance(at, int) else pl.multiple_of(at, 8)
                prod = own * padded[part, pl.ds(at, size), :]
                folded = jnp.sum(prod.reshape(size // 8, 8, LANES), axis=0)
                row = o * 8
                row = row if isinstance(row, int) else pl.multiple_of(row, 8)
                if b == 0:
                    sums[pl.ds(row, 8), lane] = folded
                else:
                    sums[pl.ds(row, 8), lane] = sums[pl.ds(row, 8), lane] + folded
                return carry

            taps_loop(0, 0, taps, one, 3)

    for t in range(taps):
        out[out_at + t : out_at + t + 1, :] = jnp.sum(sums[8 * t : 8 * t + 8, :], axis=0, keepdims=True)


def widen(src, padded, at):
    n = src.shape[0]
    for part in range(padded.shape[0]):
        lane = slice(part * LANES, (part + 1) * LANES)
        padded[part, at : at + n, :] = src[:, lane].astype(jnp.float32)


def narrow(padded, at, dst):
    n = dst.shape[0]
    for part in range(padded.shape[0]):
        lane = slice(part * LANES, (part + 1) * LANES)
        dst[:, lane] = padded[part, at : at + n, :].astype(dst.dtype)


class Halo:
    def __init__(self, at, count, target, src, low, high, sems):
        h = low.shape[0]
        top = src.shape[0] - h
        self.at, self.count, self.low, self.high = at, count, low, high
        self.up = remote(
            src.at[pl.ds(top, h)], low, sems.at[0], sems.at[1], target(lax.rem(at + 1, count))
        )
        self.down = remote(
            src.at[pl.ds(0, h)], high, sems.at[2], sems.at[3], target(lax.rem(at + count - 1, count))
        )

    def start(self):
        pl.when(self.at < self.count - 1)(self.up.start)
        pl.when(self.at > 0)(self.down.start)

    def clear(self, padded):
        h = self.low.shape[0]
        rest = padded.shape[1] - h
        zeros = jnp.zeros((padded.shape[0], h, LANES), jnp.float32)
        padded[:, 0:h, :] = zeros
        padded[:, rest : rest + h, :] = zeros

    def finish(self, padded):
        h = self.low.shape[0]
        rest = padded.shape[1] - h

        @pl.when(self.at > 0)
        def _():
            self.up.wait_recv()
            widen(self.low, padded, 0)
            self.down.wait_send()

        @pl.when(self.at < self.count - 1)
        def _():
            self.down.wait_recv()
            widen(self.high, padded, rest)
            self.up.wait_send()


def inner_range(lead, reach):
    return lambda b: [(max(reach - GROUP * b, 0), lead + reach - GROUP * b - GROUP + 1)]


def outer_range(lead, reach):
    def ranges(b):
        lo, hi = inner_range(lead, reach)(b)[0]
        return [(0, lo), (hi, 2 * reach + 1)]

    return ranges


def no_start(size):
    return lambda b, lane: jnp.zeros((size, LANES), jnp.float32)


def transposing(dst, at, inner, outer):
    def finish(b, part, lane, acc):
        value = acc.astype(jnp.bfloat16).astype(jnp.float32)
        for g in range(GROUP):
            dst[part, pl.ds(at + b * GROUP + g, inner, stride=outer), :] = value[g * inner : (g + 1) * inner]

    return finish


def into(dst, size):
    def finish(b, part, lane, acc):
        dst[pl.ds(b * size, size), lane] = acc

    return finish


def out_of(src, size):
    return lambda b, lane: src[pl.ds(b * size, size), lane]


def front_kernel(
    n_row, n_col, rows, cols, act, kw, kt, mixed, wide, tall, low_a, high_a, low_h, high_h, hid, part, sem_a, sem_h
):
    row, col = lax.axis_index("row"), lax.axis_index("col")
    barrier = pltpu.get_barrier_semaphore()
    reach = kw.shape[0] // 16
    for at, count, target in (
        (row, n_row, lambda i: (i, col)),
        (col, n_col, lambda i: (row, i)),
    ):
        pl.when(at > 0)(lambda at=at, target=target: greet(barrier, target(at - 1)))
        pl.when(at < count - 1)(lambda at=at, target=target: greet(barrier, target(at + 1)))
    greeted = below(row, n_row) + above(row, n_row) + below(col, n_col) + above(col, n_col)
    pl.semaphore_wait(barrier, greeted)
    halo = Halo(col, n_col, lambda i: (row, i), act, low_a, high_a, sem_a)
    halo.start()
    halo.clear(wide)
    widen(act, wide, reach * rows)
    blocks, size = range(cols // GROUP), GROUP * rows
    conv_pass(wide, kw, False, rows, inner_range(cols, reach), blocks, no_start(size), into(part, size))
    halo.finish(wide)
    conv_pass(
        wide, kw, False, rows, outer_range(cols, reach), blocks, out_of(part, size),
        transposing(tall, reach * cols, rows, cols),
    )
    narrow(tall, reach * cols, hid)
    halo = Halo(row, n_row, lambda i: (i, col), hid, low_h, high_h, sem_h)
    halo.start()
    halo.clear(tall)
    blocks, size = range(rows // GROUP), GROUP * cols
    conv_pass(tall, kt, False, cols, inner_range(rows, reach), blocks, no_start(size), into(part, size))
    halo.finish(tall)
    conv_pass(
        tall, kt, False, cols, outer_range(rows, reach), blocks, out_of(part, size), into(mixed, size)
    )


class Net:
    def __init__(self, n_row, n_col, factor, src, scratch):
        self.src, self.n_col, self.factor = src, n_col, factor
        self.pair_buf, self.half, self.slots, self.cols, self.whole = scratch[:5]
        self.sems = scratch[5:]
        self.row, self.col = lax.axis_index("row"), lax.axis_index("col")
        self.m = n_row // 2
        self.core, self.j = lax.rem(self.row, 2), self.row // 2
        self.pair = (self.row + 1 - 2 * self.core, self.col)
        self.p = self.slots.shape[1]
        self.h = self.half.shape[0]

    def peer(self, d):
        return (2 * lax.rem(self.j + d, self.m) + self.core, self.col)

    def col_peer(self, d):
        return (self.row, lax.rem(self.col + d, self.n_col))

    def pair_copy(self):
        other = pl.multiple_of((1 - self.core) * self.h, 16)
        return remote(self.src.at[pl.ds(other, self.h)], self.pair_buf, self.sems[0], self.sems[1], self.pair)

    def peer_copy(self, d):
        at = pl.multiple_of(lax.rem(self.j + d, self.m) * self.p, self.p)
        return remote(
            self.half.at[pl.ds(at, self.p)], self.slots.at[d], self.sems[2].at[d], self.sems[3].at[d], self.peer(d)
        )

    def col_copy(self, d, c):
        return remote(self.cols.at[c], self.cols.at[c], self.sems[4].at[d], self.sems[5].at[c], self.col_peer(d))

    def back_copy(self, d, owner):
        at = pl.multiple_of(self.core * self.h + owner * self.p, self.p)
        part = self.whole.at[pl.ds(at, self.p)]
        return remote(part, part, self.sems[6].at[d], self.sems[7].at[d], self.peer(d))

    def last_copy(self, side):
        part = self.whole.at[pl.ds(pl.multiple_of(side * self.h, 16), self.h)]
        return remote(part, part, self.sems[8], self.sems[9], self.pair)

    def step_pair(self):
        self.pair_copy().start()

    def step_peers(self):
        self.pair_copy().wait()
        at = pl.multiple_of(self.core * self.h, 16)
        mine = self.src[pl.ds(at, self.h), :].astype(jnp.float32)
        self.half[...] = (mine + self.pair_buf[...].astype(jnp.float32)).astype(self.half.dtype)

        @pl.loop(1, self.m)
        def _(d):
            self.peer_copy(d).start()

    def step_cols(self):
        at = pl.multiple_of(self.j * self.p, self.p)
        self.cols[self.col] = self.half[pl.ds(at, self.p), :].astype(jnp.float32)

        @pl.loop(1, self.m)
        def _(d):
            self.peer_copy(d).wait()
            self.cols[self.col] = self.cols[self.col] + self.slots[d].astype(jnp.float32)

        @pl.loop(1, self.n_col)
        def _(d):
            self.col_copy(d, self.col).start()

    def step_back(self):
        @pl.loop(1, self.n_col)
        def _(d):
            self.col_copy(d, self.col).wait_send()
            self.col_copy(d, lax.rem(self.col + d, self.n_col)).wait_recv()

        total = self.cols[0]
        for c in range(1, self.n_col):
            total = total + self.cols[c]
        at = pl.multiple_of(self.core * self.h + self.j * self.p, self.p)
        self.whole[pl.ds(at, self.p), :] = (total * self.factor).astype(self.whole.dtype)

        @pl.loop(1, self.m)
        def _(d):
            self.back_copy(d, self.j).start()

    def step_last(self):
        @pl.loop(1, self.m)
        def _(d):
            self.back_copy(d, self.j).wait_send()
            self.back_copy(d, lax.rem(self.j + self.m - d, self.m)).wait_recv()

        self.last_copy(self.core).start()

    def step_end(self):
        self.last_copy(self.core).wait_send()
        self.last_copy(1 - self.core).wait_recv()


def back_kernel(
    n_row, n_col, rows, cols, factor, gm, tall, wide, kw, kt, big, gin, in_out, out_out, small_out,
    gpad, hpad, low_g, high_g, low_h, high_h, ghb, part, sums, small, sem_g, sem_h, *scratch
):
    row, col = lax.axis_index("row"), lax.axis_index("col")
    reach, taps = kw.shape[0] // 16, kw.shape[0] // 8
    net = Net(n_row, n_col, factor, big, scratch[:15])
    net2 = Net(n_row, n_col, factor, small, scratch[15:])
    barrier = pltpu.get_barrier_semaphore()
    other = row - 1 + 2 * net.core
    present = jnp.logical_and(other >= 0, other < n_row)
    greet(barrier, net.pair)
    pl.when(present)(lambda: greet(barrier, (other, col)))

    @pl.loop(1, net.m)
    def _(d):
        greet(barrier, net.peer(d))

    @pl.loop(1, n_col)
    def _(d):
        greet(barrier, net.col_peer(d))

    more = (1 - net.core) * below(row, n_row) + net.core * above(row, n_row)
    pl.semaphore_wait(barrier, 1 + (net.m - 1) + (n_col - 1) + more)

    halo = Halo(row, n_row, lambda i: (i, col), gm, low_g, high_g, sem_g)
    halo.start()
    net.step_pair()
    halo.clear(gpad)
    widen(gm, gpad, reach * cols)
    small[2 * taps :, :] = jnp.zeros((small.shape[0] - 2 * taps, small.shape[1]), jnp.float32)
    correlate(reach * cols, gpad, tall, taps, cols, sums, small, taps)
    halo.finish(gpad)
    net.step_peers()
    blocks, size = range(rows // GROUP), GROUP * cols
    conv_pass(
        gpad, kt, True, cols, lambda b: [(0, taps)], blocks, no_start(size),
        transposing(hpad, reach * rows, cols, rows),
    )
    narrow(hpad, reach * rows, ghb)
    halo = Halo(col, n_col, lambda i: (row, i), ghb, low_h, high_h, sem_h)
    halo.start()
    halo.clear(hpad)
    correlate(reach * rows, hpad, wide, taps, rows, sums, small, 0)
    net2.step_pair()
    net.step_cols()
    blocks, size = range(cols // GROUP), GROUP * rows
    conv_pass(hpad, kw, True, rows, inner_range(cols, reach), blocks, no_start(size), into(part, size))
    net2.step_peers()
    halo.finish(hpad)
    net.step_back()
    half = len(blocks) // 2
    outer = outer_range(cols, reach)
    conv_pass(hpad, kw, True, rows, outer, blocks[:half], out_of(part, size), into(gin, size))
    net2.step_cols()
    conv_pass(hpad, kw, True, rows, outer, blocks[half:], out_of(part, size), into(gin, size))
    net2.step_back()
    net.step_last()
    net2.step_last()
    net.step_end()
    net2.step_end()
    depth, width = in_out.shape[0], net.whole.shape[1]
    inner = in_out.shape[1] // width
    for b in range(inner):
        in_out[:, b * width : (b + 1) * width] = net.whole[b * depth : (b + 1) * depth, :]
    out_out[...] = net.whole[inner * depth :, :]
    small_out[...] = net2.whole[...]


def net_scratch(src, n_row, n_col):
    rows, width = src.shape
    p, m = rows // n_row, n_row // 2
    dma = pltpu.SemaphoreType.DMA
    return [
        pltpu.VMEM((rows // 2, width), src.dtype),
        pltpu.VMEM((rows // 2, width), src.dtype),
        pltpu.VMEM((m, p, width), src.dtype),
        pltpu.VMEM((n_col, p, width), jnp.float32),
        pltpu.VMEM((rows, width), src.dtype),
        dma, dma, dma((m,)), dma((m,)), dma((n_col,)), dma((n_col,)), dma((m,)), dma((m,)), dma, dma,
    ]


def params(number):
    return pltpu.CompilerParams(
        collective_id=number, has_side_effects=True, vmem_limit_bytes=40 * 1024 * 1024
    )


def local(
    activations, cotangent, kernel_wide, kernel_tall, norm_gain, norm_bias, weight_in, bias_in, weight_out, layer_scale
):
    rows, cols, chans = activations.shape
    taps = kernel_wide.shape[0]
    reach = taps // 2
    n_row, n_col = lax.axis_size("row"), lax.axis_size("col")
    pixels = rows * cols
    f32, bf16 = jnp.float32, jnp.bfloat16
    vmem = pl.BlockSpec(memory_space=pltpu.VMEM)
    dma = pltpu.SemaphoreType.DMA
    wide_shape = jax.ShapeDtypeStruct((chans // LANES, (cols + 2 * reach) * rows, LANES), f32)
    tall_shape = jax.ShapeDtypeStruct((chans // LANES, (rows + 2 * reach) * cols, LANES), f32)
    halos = [
        pltpu.VMEM((reach * rows, chans), bf16),
        pltpu.VMEM((reach * rows, chans), bf16),
        pltpu.VMEM((reach * cols, chans), bf16),
        pltpu.VMEM((reach * cols, chans), bf16),
    ]
    tile = [pltpu.VMEM((pixels, chans), bf16), pltpu.VMEM((pixels, chans), f32)]
    kw, kt = jnp.repeat(kernel_wide, 8, axis=0), jnp.repeat(kernel_tall, 8, axis=0)
    act_flat = activations.transpose(1, 0, 2).reshape(pixels, chans)
    mixed, wide, tall = pl.pallas_call(
        functools.partial(front_kernel, n_row, n_col, rows, cols),
        out_shape=(jax.ShapeDtypeStruct((pixels, chans), f32), wide_shape, tall_shape),
        in_specs=[vmem] * 3,
        out_specs=(vmem,) * 3,
        scratch_shapes=halos + tile + [dma((4,)), dma((4,))],
        compiler_params=params(0),
    )(act_flat, kw, kt)
    grad_mixed, sum_in, sum_out = mlp_backward(
        mixed,
        cotangent.reshape(pixels, chans),
        norm_gain, norm_bias, weight_in, bias_in, weight_out, layer_scale,
    )
    factor = 1.0 / math.sqrt(pixels * n_row * n_col)
    hidden_units = weight_in.shape[1]
    big = jnp.concatenate(
        [sum_in[:, b : b + chans] for b in range(0, hidden_units, chans)] + [sum_out], axis=0
    ).astype(bf16)
    each = -(-2 * taps // (8 * n_row)) * 8
    small = jax.ShapeDtypeStruct((each * n_row, chans), f32)
    grad_flat, grad_in, grad_out, tapped = pl.pallas_call(
        functools.partial(back_kernel, n_row, n_col, rows, cols, factor),
        out_shape=(
            jax.ShapeDtypeStruct((pixels, chans), f32),
            jax.ShapeDtypeStruct(sum_in.shape, bf16),
            jax.ShapeDtypeStruct(sum_out.shape, bf16),
            small,
        ),
        in_specs=[vmem] * 6,
        out_specs=(vmem,) * 4,
        scratch_shapes=[pltpu.VMEM(tall_shape.shape, f32), pltpu.VMEM(wide_shape.shape, f32)]
        + halos[2:] + halos[:2] + tile
        + [pltpu.VMEM((8 * taps, chans), f32), pltpu.VMEM(small.shape, f32), dma((4,)), dma((4,))]
        + net_scratch(big, n_row, n_col)
        + net_scratch(small, n_row, n_col),
        compiler_params=params(1),
    )(grad_mixed, tall, wide, kw, kt, big)
    spread = grad_flat.reshape(cols, rows, chans).transpose(1, 0, 2)
    grad_input = (cotangent.astype(f32) + spread).astype(bf16)
    return (grad_input, grad_in, grad_out, tapped[:taps], tapped[taps : 2 * taps])


def solution(mesh):
    in_specs = (
        P("row", "col", None),
        P("row", "col", None),
        P(),
        P(),
        P(),
        P(),
        P(),
        P(),
        P(),
        P(),
    )
    out_specs = (P("row", "col", None), P(), P(), P(), P())
    return jax.shard_map(local, mesh=mesh, in_specs=in_specs, out_specs=out_specs, check_vma=False)
```

time: 423 us -> 99.5 us (0.24)
  waiting for transfers between devices: 244 us -> 0 us
  other arithmetic: 94 us -> 4.05 us
  Pallas kernels: 0 us -> 78.1 us
  starting transfers between devices: 25.2 us -> 0 us
  local copies, waits for them, and re-layouts: 28.5 us -> 8.25 us
  between operations: 16 us -> 0.87 us
  matrix products: 13.2 us -> 7.85 us
    psum x2 -> x0, waiting for transfers between devices: 237 us -> none  [local(): lax.psum((sum_in, sum_out, part_wide, part_tall), ('row', 'col'))]
    pallas_call x0 -> x2, Pallas kernels: none -> 78.1 us  [the longest x1 56.4 us: local(): pl.pallas_call(functools.partial(back_kernel, n_row, n_col, rows, cols, f...]
    reduce_sum x11 -> x0, other arithmetic: 45.2 us -> none  [the longest x5 27.9 us: correlate_columns(): jnp.sum(gradf * padded[:, offset:offset + length, :].astype(jnp.float32),...]
    convert_element_type x5 -> x2, other arithmetic: 30 us -> 2.25 us  [the longest x1 1.39 us: local(): grad_input = (cotangent.astype(f32) + spread).astype(bf16)]
    ppermute x8 -> x0, starting transfers between devices: 24.9 us -> none  [the longest x4 19.6 us: with_halo(): lax.ppermute(lax.slice_in_dim(block, block.shape[dim] - width, None, axis...]
    another operation x2 -> x0, local copies, waits for them, and re-layouts: 13.5 us -> none  [the longest x1 9.19 us: correlate_rows(): jnp.stack([jnp.sum(gradf * padded[offset:offset + length].astype(jnp.floa...]
    reduce_sum x1, other arithmetic: 13.4 us -> 0.21 us  [mlp_backward(): average = jnp.mean(mixed, axis=-1, keepdims=True)]
    slice x10 -> x1, local copies, waits for them, and re-layouts: 11.6 us -> 0.65 us  [local(): return (grad_input, grad_in, grad_out, tapped[:taps], tapped[taps:2 * taps])]
  transfers between devices with their start and end apart: 10 -> 0, of which waited for: 4 -> 0; matrix products, arithmetic and copies ran while one was open for 13% -> 0% of each run, Pallas kernels for 0% -> 0%
where the time goes in v2:
time: 99.5 us; the launch traced here: 99.1 us
  Pallas kernels  78.1 us (78%)
  local copies, waits for them, and re-layouts  8.25 us (8%)
  matrix products  7.85 us (8%)
  other arithmetic  4.05 us (4%)
    pallas_call x1, Pallas kernels, local(): pl.pallas_call(functools.partial(back_kernel, n_row, n_col, rows, cols, f...  56.4 us
    pallas_call x1, Pallas kernels, local(): pl.pallas_call(functools.partial(front_kernel, n_row, n_col, rows, cols),...  21.7 us
    unnamed x26, local copies, waits for them, and re-layouts  5.36 us
    dot_general x1, matrix products, mlp_backward(): jnp.dot(scaled_cot, weight_out.T, preferred_element_type=jnp.float32)  3.27 us

profile of v2, /device:TPU:0, one launch (start us, length us, event | category | flops | bytes accessed | tf_op | source)
XLA Modules:
  0.0 99.1 jit_solution(12552983261768729124)
XLA Ops:
  0.6 0.0 copy-start
  0.6 0.0 copy-start.7
  0.7 0.0 copy-start.6
  0.7 1.2 %fusion.11 = bf16[1024,256]{1,0:T(8,128)(2,1)S(1)} fusion(f32[256]{0:T(256)} %param.19, bf16[32,32,256]{2,1,0:T(8,128)(2,1)} %param.11), kind=kLoop, calls=%fused_computation.18 | loop fusion | flops 786432 | bytes 1049600 | tf_op jit(solution)/shard_map/convert_element_type | solution.py:26
  1.9 1.3 %copy.15 = bf16[32,32,256]{2,1,0:T(8,128)(2,1)S(1)} copy(bf16[32,32,256]{2,0,1:T(8,128)(2,1)} %bitcast.24) | data formatting | bytes 1048576 | tf_op jit(solution)/shard_map/transpose | solution.py:460
  3.2 0.9 broadcast_bitcast_fusion
  4.1 21.7 %shard_map.137 = (f32[1024,256]{1,0:T(8,128)S(1)}, f32[2,2624,128]{2,1,0:T(8,128)S(1)}, f32[2,2624,128]{2,1,0:T(8,128)S(1)}) custom-call(bf16[1024,256]{1,0:T(8,128)(2,1)S(1)} %bitcast.22, f32[408,256]{1,0:T(8,128)S(1)} %get-tuple-element.25.kw, f32[408,256]{1,0:T(8,128)S(1)} %get-tuple-element.24.kt), custom_call_target="tpu_custom_call" | custom-call | tf_op jit(solution)/shard_map/pallas_call | solution.py:461
  25.8 0.0 copy-start.1
  25.8 1.5 %copy-done.1 = f32[2,2624,128]{2,1,0:T(8,128)} copy-done((f32[2,2624,128]{2,1,0:T(8,128)}, f32[2,2624,128]{2,1,0:T(8,128)S(1)}, u32[]{:S(2)}) %copy-start.1) | copy-done | bytes 2687000
  27.3 0.0 copy-start.3
  27.3 1.5 %copy-done.3 = f32[2,2624,128]{2,1,0:T(8,128)} copy-done((f32[2,2624,128]{2,1,0:T(8,128)}, f32[2,2624,128]{2,1,0:T(8,128)S(1)}, u32[]{:S(2)}) %copy-start.3) | copy-done | bytes 2687000
  28.9 0.0 copy-start.8
  28.9 0.0 copy-start.9
  28.9 0.2 reduce_sum.36
  29.1 0.4 multiply_reduce_fusion.1
  29.5 0.0 copy-done
  29.5 0.0 copy-done.7
  29.5 0.0 copy-done.6
  29.5 0.8 fusion.16
  30.3 0.0 copy-done.8
  30.3 0.0 copy-done.9
  30.3 3.3 %fusion.6 = bf16[1024,1024]{1,0:T(8,128)(2,1)S(1)} fusion(f32[1024,1024]{1,0:T(8,128)S(1)} %fusion.16, bf16[1024,256]{1,0:T(8,128)(2,1)S(1)} %fusion.11, bf16[1024,256]{1,0:T(8,128)(2,1)S(1)} %copy-done.8, f32[1024]{0:T(1024)S(1)} %copy-done.9), kind=kOutput, calls=%fused_computation.8 | convolution fusion | flops 558891008 | bytes 7344128 | tf_op jit(solution)/shard_map/dot_general | solution.py:28
  33.6 1.0 %convolution_convert_fusion = bf16[256,1024]{1,0:T(8,128)(2,1)S(1)} fusion(bf16[1024,1024]{1,0:T(8,128)(2,1)S(1)} %fusion.6, f32[1024,256]{1,0:T(8,128)S(1)} %get-tuple-element.12, f32[256]{0:T(256)S(1)} %copy-done.6, f32[256]{0:T(256)S(1)} %copy-done.7, f32[1024]{0:T(1024)S(1)} %add_rsqrt_fusion, f32[1024]{0:T(1024)S(1)} %broadcast_multiply_fusion.2), kind=kOutput, calls=%fused_computation.12 | convolution fusion | flops 538443776 | bytes 3680256 | tf_op jit(solution)/shard_map/dot_general | solution.py:30
  34.6 0.9 fusion.17
  35.5 0.9 multiply_convert_fusion.6.gm
  36.5 0.0 copy-start.2
  36.5 0.0 copy-start.4
  36.5 1.9 %fusion.9.big = bf16[2048,256]{1,0:T(8,128)(2,1)S(1)} fusion(bf16[2048,256]{1,0:T(8,128)(2,1)S(1)} %slice_dynamic-update-slice_fusion, bf16[1024,256]{1,0:T(8,128)(2,1)S(1)} %fusion.11, f32[1024,1024]{1,0:T(8,128)S(1)} %fusion.16, f32[1024]{0:T(1024)S(1)} %copy-done.9), kind=kOutput, calls=%fused_computation.14 | convolution fusion | flops 547618816 | bytes 5246976 | tf_op jit(solution)/shard_map/dot_general | solution.py:27
  38.4 0.0 copy-done.2
  38.4 0.6 copy-done.4
  39.0 0.0 copy-start.5
  39.0 56.4 %shard_map.138 = (f32[1024,256]{1,0:T(8,128)S(1)}, bf16[256,1024]{1,0:T(8,128)(2,1)S(1)}, bf16[1024,256]{1,0:T(8,128)(2,1)S(1)}, f32[128,256]{1,0:T(8,128)S(1)}) custom-call(bf16[1024,256]{1,0:T(8,128)(2,1)S(1)} %multiply_convert_fusion.6.gm, f32[2,2624,128]{2,1,0:T(8,128)S(1)} %copy-done.4, f32[2,2624,128]{2,1,0:T(8,128)S(1)} %copy-done.2, ...), custom_call_target="tpu_custom_call" | custom-call | tf_op jit(solution)/shard_map/pallas_call | solution.py:481
  95.5 0.0 copy-done.5
  95.5 1.4 %fusion.10 = bf16[32,32,256]{2,1,0:T(8,128)(2,1)} fusion(f32[32,32,256]{2,1,0:T(8,128)S(1)} %bitcast.23, bf16[32,32,256]{2,1,0:T(8,128)(2,1)S(1)} %copy-done.5), kind=kLoop, calls=%fused_computation.16 | loop fusion | flops 786432 | bytes 2097152 | tf_op jit(solution)/shard_map/convert_element_type | solution.py:499
  96.8 0.7 fusion.18
  97.5 0.8 copy.26
  98.3 0.8 copy.27
  (8 shorter events, 0.1 us)
Async XLA Ops:
  0.6 28.8 %copy-start = (bf16[256,1024]{1,0:T(8,128)(2,1)S(1)}, bf16[256,1024]{1,0:T(8,128)(2,1)}, u32[]{:S(2)}) copy-start(bf16[256,1024]{1,0:T(8,128)(2,1)} %param.16) | copy-start | bytes 1572868
  0.6 28.8 %copy-start.7 = (f32[256]{0:T(256)S(1)}, f32[256]{0:T(256)}, u32[]{:S(2)}) copy-start(f32[256]{0:T(256)} %param.14) | copy-start | bytes 3076
  0.7 28.8 %copy-start.6 = (f32[256]{0:T(256)S(1)}, f32[256]{0:T(256)}, u32[]{:S(2)}) copy-start(f32[256]{0:T(256)} %param.15) | copy-start | bytes 3076
  25.8 1.5 %copy-start.1 = (f32[2,2624,128]{2,1,0:T(8,128)}, f32[2,2624,128]{2,1,0:T(8,128)S(1)}, u32[]{:S(2)}) copy-start(f32[2,2624,128]{2,1,0:T(8,128)S(1)} %get-tuple-element.14.wide) | copy-start | bytes 8060932
  27.3 1.5 %copy-start.3 = (f32[2,2624,128]{2,1,0:T(8,128)}, f32[2,2624,128]{2,1,0:T(8,128)S(1)}, u32[]{:S(2)}) copy-start(f32[2,2624,128]{2,1,0:T(8,128)S(1)} %get-tuple-element.13.tall) | copy-start | bytes 8060932
  28.9 1.4 %copy-start.8 = (bf16[1024,256]{1,0:T(8,128)(2,1)S(1)}, bf16[1024,256]{1,0:T(8,128)(2,1)}, u32[]{:S(2)}) copy-start(bf16[1024,256]{1,0:T(8,128)(2,1)} %param.18) | copy-start | bytes 1572868
  28.9 1.4 %copy-start.9 = (f32[1024]{0:T(1024)S(1)}, f32[1024]{0:T(1024)}, u32[]{:S(2)}) copy-start(f32[1024]{0:T(1024)} %param.17) | copy-start | bytes 12292
  36.5 2.0 %copy-start.2 = (f32[2,2624,128]{2,1,0:T(8,128)S(1)}, f32[2,2624,128]{2,1,0:T(8,128)}, u32[]{:S(2)}) copy-start(f32[2,2624,128]{2,1,0:T(8,128)} %copy-done.1) | copy-start | bytes 8060932
  36.5 2.6 %copy-start.4 = (f32[2,2624,128]{2,1,0:T(8,128)S(1)}, f32[2,2624,128]{2,1,0:T(8,128)}, u32[]{:S(2)}) copy-start(f32[2,2624,128]{2,1,0:T(8,128)} %copy-done.3) | copy-start | bytes 8060932
  39.0 56.4 %copy-start.5 = (bf16[32,32,256]{2,1,0:T(8,128)(2,1)S(1)}, bf16[32,32,256]{2,1,0:T(8,128)(2,1)}, u32[]{:S(2)}) copy-start(bf16[32,32,256]{2,1,0:T(8,128)(2,1)} %param.11) | copy-start | bytes 1572868

commit v3 on v2

--- a/solution.py
+++ b/solution.py
@@ -378,26 +378,26 @@
     halo.clear(gpad)
     widen(gm, gpad, reach * cols)
     small[2 * taps :, :] = jnp.zeros((small.shape[0] - 2 * taps, small.shape[1]), jnp.float32)
+    net.step_peers()
     correlate(reach * cols, gpad, tall, taps, cols, sums, small, taps)
     halo.finish(gpad)
-    net.step_peers()
     blocks, size = range(rows // GROUP), GROUP * cols
     conv_pass(
         gpad, kt, True, cols, lambda b: [(0, taps)], blocks, no_start(size),
         transposing(hpad, reach * rows, cols, rows),
     )
+    net.step_cols()
     narrow(hpad, reach * rows, ghb)
     halo = Halo(col, n_col, lambda i: (row, i), ghb, low_h, high_h, sem_h)
     halo.start()
     halo.clear(hpad)
     correlate(reach * rows, hpad, wide, taps, rows, sums, small, 0)
     net2.step_pair()
-    net.step_cols()
+    net.step_back()
     blocks, size = range(cols // GROUP), GROUP * rows
     conv_pass(hpad, kw, True, rows, inner_range(cols, reach), blocks, no_start(size), into(part, size))
     net2.step_peers()
     halo.finish(hpad)
-    net.step_back()
     half = len(blocks) // 2
     outer = outer_range(cols, reach)
     conv_pass(hpad, kw, True, rows, outer, blocks[:half], out_of(part, size), into(gin, size))

time: 99.5 us -> 106 us (1.065)
  Pallas kernels: 78.1 us -> 84.7 us
    pallas_call x1, Pallas kernels: 56.4 us -> 63 us  [local(): pl.pallas_call(functools.partial(back_kernel, n_row, n_col, rows, cols, f...]
where the time goes in v3:
time: 106 us
  Pallas kernels  84.7 us (80%)
  local copies, waits for them, and re-layouts  8.25 us (8%)
  matrix products  7.85 us (7%)
  other arithmetic  4.05 us (4%)
    pallas_call x1, Pallas kernels, local(): pl.pallas_call(functools.partial(back_kernel, n_row, n_col, rows, cols, f...  63 us
    pallas_call x1, Pallas kernels, local(): pl.pallas_call(functools.partial(front_kernel, n_row, n_col, rows, cols),...  21.7 us
    unnamed x26, local copies, waits for them, and re-layouts  5.36 us
    dot_general x1, matrix products, mlp_backward(): jnp.dot(scaled_cot, weight_out.T, preferred_element_type=jnp.float32)  3.27 us

profile of v3, /device:TPU:0, one launch (start us, length us, event | category | flops | bytes accessed | tf_op | source)
XLA Modules:
  0.0 105.7 jit_solution(5342113347510770862)
XLA Ops:
  0.6 0.0 copy-start
  0.6 0.0 copy-start.7
  0.7 0.0 copy-start.6
  0.7 1.2 %fusion.11 = bf16[1024,256]{1,0:T(8,128)(2,1)S(1)} fusion(f32[256]{0:T(256)} %param.19, bf16[32,32,256]{2,1,0:T(8,128)(2,1)} %param.11), kind=kLoop, calls=%fused_computation.18 | loop fusion | flops 786432 | bytes 1049600 | tf_op jit(solution)/shard_map/convert_element_type | solution.py:26
  1.9 1.3 %copy.15 = bf16[32,32,256]{2,1,0:T(8,128)(2,1)S(1)} copy(bf16[32,32,256]{2,0,1:T(8,128)(2,1)} %bitcast.24) | data formatting | bytes 1048576 | tf_op jit(solution)/shard_map/transpose | solution.py:460
  3.2 0.9 broadcast_bitcast_fusion
  4.1 21.7 %shard_map.137 = (f32[1024,256]{1,0:T(8,128)S(1)}, f32[2,2624,128]{2,1,0:T(8,128)S(1)}, f32[2,2624,128]{2,1,0:T(8,128)S(1)}) custom-call(bf16[1024,256]{1,0:T(8,128)(2,1)S(1)} %bitcast.22, f32[408,256]{1,0:T(8,128)S(1)} %get-tuple-element.25.kw, f32[408,256]{1,0:T(8,128)S(1)} %get-tuple-element.24.kt), custom_call_target="tpu_custom_call" | custom-call | tf_op jit(solution)/shard_map/pallas_call | solution.py:461
  25.8 0.0 copy-start.1
  25.8 1.5 %copy-done.1 = f32[2,2624,128]{2,1,0:T(8,128)} copy-done((f32[2,2624,128]{2,1,0:T(8,128)}, f32[2,2624,128]{2,1,0:T(8,128)S(1)}, u32[]{:S(2)}) %copy-start.1) | copy-done | bytes 2687000
  27.3 0.0 copy-start.3
  27.3 1.5 %copy-done.3 = f32[2,2624,128]{2,1,0:T(8,128)} copy-done((f32[2,2624,128]{2,1,0:T(8,128)}, f32[2,2624,128]{2,1,0:T(8,128)S(1)}, u32[]{:S(2)}) %copy-start.3) | copy-done | bytes 2687000
  28.9 0.0 copy-start.8
  28.9 0.0 copy-start.9
  28.9 0.2 reduce_sum.36
  29.1 0.4 multiply_reduce_fusion.1
  29.5 0.0 copy-done
  29.5 0.0 copy-done.7
  29.5 0.0 copy-done.6
  29.5 0.8 fusion.16
  30.3 0.0 copy-done.8
  30.3 0.0 copy-done.9
  30.3 3.3 %fusion.6 = bf16[1024,1024]{1,0:T(8,128)(2,1)S(1)} fusion(f32[1024,1024]{1,0:T(8,128)S(1)} %fusion.16, bf16[1024,256]{1,0:T(8,128)(2,1)S(1)} %fusion.11, bf16[1024,256]{1,0:T(8,128)(2,1)S(1)} %copy-done.8, f32[1024]{0:T(1024)S(1)} %copy-done.9), kind=kOutput, calls=%fused_computation.8 | convolution fusion | flops 558891008 | bytes 7344128 | tf_op jit(solution)/shard_map/dot_general | solution.py:28
  33.6 1.0 convolution_convert_fusion
  34.6 0.9 fusion.17
  35.5 0.9 multiply_convert_fusion.6.gm
  36.5 0.0 copy-start.2
  36.5 0.0 copy-start.4
  36.5 1.9 %fusion.9.big = bf16[2048,256]{1,0:T(8,128)(2,1)S(1)} fusion(bf16[2048,256]{1,0:T(8,128)(2,1)S(1)} %slice_dynamic-update-slice_fusion, bf16[1024,256]{1,0:T(8,128)(2,1)S(1)} %fusion.11, f32[1024,1024]{1,0:T(8,128)S(1)} %fusion.16, f32[1024]{0:T(1024)S(1)} %copy-done.9), kind=kOutput, calls=%fused_computation.14 | convolution fusion | flops 547618816 | bytes 5246976 | tf_op jit(solution)/shard_map/dot_general | solution.py:27
  38.4 0.0 copy-done.2
  38.4 0.6 copy-done.4
  39.0 0.0 copy-start.5
  39.0 63.0 %shard_map.138 = (f32[1024,256]{1,0:T(8,128)S(1)}, bf16[256,1024]{1,0:T(8,128)(2,1)S(1)}, bf16[1024,256]{1,0:T(8,128)(2,1)S(1)}, f32[128,256]{1,0:T(8,128)S(1)}) custom-call(bf16[1024,256]{1,0:T(8,128)(2,1)S(1)} %multiply_convert_fusion.6.gm, f32[2,2624,128]{2,1,0:T(8,128)S(1)} %copy-done.4, f32[2,2624,128]{2,1,0:T(8,128)S(1)} %copy-done.2, ...), custom_call_target="tpu_custom_call" | custom-call | tf_op jit(solution)/shard_map/pallas_call | solution.py:481
  102.0 0.0 copy-done.5
  102.1 1.4 %fusion.10 = bf16[32,32,256]{2,1,0:T(8,128)(2,1)} fusion(f32[32,32,256]{2,1,0:T(8,128)S(1)} %bitcast.23, bf16[32,32,256]{2,1,0:T(8,128)(2,1)S(1)} %copy-done.5), kind=kLoop, calls=%fused_computation.16 | loop fusion | flops 786432 | bytes 2097152 | tf_op jit(solution)/shard_map/convert_element_type | solution.py:499
  103.4 0.7 fusion.18
  104.1 0.8 copy.26
  104.9 0.8 copy.27
  (8 shorter events, 0.1 us)
Async XLA Ops:
  0.6 28.8 %copy-start = (bf16[256,1024]{1,0:T(8,128)(2,1)S(1)}, bf16[256,1024]{1,0:T(8,128)(2,1)}, u32[]{:S(2)}) copy-start(bf16[256,1024]{1,0:T(8,128)(2,1)} %param.16) | copy-start | bytes 1572868
  0.6 28.8 %copy-start.7 = (f32[256]{0:T(256)S(1)}, f32[256]{0:T(256)}, u32[]{:S(2)}) copy-start(f32[256]{0:T(256)} %param.14) | copy-start | bytes 3076
  0.7 28.8 %copy-start.6 = (f32[256]{0:T(256)S(1)}, f32[256]{0:T(256)}, u32[]{:S(2)}) copy-start(f32[256]{0:T(256)} %param.15) | copy-start | bytes 3076
  25.8 1.5 %copy-start.1 = (f32[2,2624,128]{2,1,0:T(8,128)}, f32[2,2624,128]{2,1,0:T(8,128)S(1)}, u32[]{:S(2)}) copy-start(f32[2,2624,128]{2,1,0:T(8,128)S(1)} %get-tuple-element.14.wide) | copy-start | bytes 8060932
  27.3 1.5 %copy-start.3 = (f32[2,2624,128]{2,1,0:T(8,128)}, f32[2,2624,128]{2,1,0:T(8,128)S(1)}, u32[]{:S(2)}) copy-start(f32[2,2624,128]{2,1,0:T(8,128)S(1)} %get-tuple-element.13.tall) | copy-start | bytes 8060932
  28.9 1.4 %copy-start.8 = (bf16[1024,256]{1,0:T(8,128)(2,1)S(1)}, bf16[1024,256]{1,0:T(8,128)(2,1)}, u32[]{:S(2)}) copy-start(bf16[1024,256]{1,0:T(8,128)(2,1)} %param.18) | copy-start | bytes 1572868
  28.9 1.4 %copy-start.9 = (f32[1024]{0:T(1024)S(1)}, f32[1024]{0:T(1024)}, u32[]{:S(2)}) copy-start(f32[1024]{0:T(1024)} %param.17) | copy-start | bytes 12292
  36.5 2.0 %copy-start.2 = (f32[2,2624,128]{2,1,0:T(8,128)S(1)}, f32[2,2624,128]{2,1,0:T(8,128)}, u32[]{:S(2)}) copy-start(f32[2,2624,128]{2,1,0:T(8,128)} %copy-done.1) | copy-start | bytes 8060932
  36.5 2.6 %copy-start.4 = (f32[2,2624,128]{2,1,0:T(8,128)S(1)}, f32[2,2624,128]{2,1,0:T(8,128)}, u32[]{:S(2)}) copy-start(f32[2,2624,128]{2,1,0:T(8,128)} %copy-done.3) | copy-start | bytes 8060932
  39.0 63.0 %copy-start.5 = (bf16[32,32,256]{2,1,0:T(8,128)(2,1)S(1)}, bf16[32,32,256]{2,1,0:T(8,128)(2,1)}, u32[]{:S(2)}) copy-start(bf16[32,32,256]{2,1,0:T(8,128)(2,1)} %param.11) | copy-start | bytes 1572868
